TPU v7x, 128 devices: a whole 4x4x4 slice. The times are simulated.
128 devices in a mesh: row: 8 (over y, core), col: 16 (over x, z).
Axes of the slice: x: 4, y: 4, z: 4, core: 2. Of those that a mesh axis runs over, the one named last changes fastest.
Arguments:
- tokens: bfloat16 [256, 768, 512], P('row', 'col'), may hold values from -6 to 6
- cloud_mask: int32 [16, 48], P('row', 'col'), may hold values from 0 to 1, as said below
- w_qkv: bfloat16 [2, 512, 1536], replicated, may hold values from -1 to 1
- b_qkv: float32 [2, 1536], replicated, may hold values from -2 to 2
- w_proj: bfloat16 [2, 512, 512], replicated, may hold values from -0.25 to 0.25
- b_proj: float32 [2, 512], replicated, may hold values from -3 to 3
- w_up: bfloat16 [2, 512, 2048], replicated, may hold values from -0.25 to 0.25
- b_up: float32 [2, 2048], replicated, may hold values from -3 to 3
- w_down: bfloat16 [2, 2048, 512], replicated, may hold values from -0.125 to 0.125
- b_down: float32 [2, 512], replicated, may hold values from -3 to 3
- norm_gain: float32 [2, 2, 512], replicated, may hold values from 0.5 to 1.5
- norm_shift: float32 [2, 2, 512], replicated, may hold values from -2 to 2
- logit_scale: float32 [2, 16], replicated, may hold values from 4 to 40
- position_table: float32 [2, 16, 961], replicated, may hold values from 0 to 16
Outputs:
- encoded: bfloat16 [256, 768, 512], P('row', 'col')
Inputs may be any that keep to these rules, and one draw needn't show every extreme that they name: `cloud_mask`: the windows of each row of tiles (2 window rows across the whole image) include exactly 48 clear ones.
All inputs are finite; a program needn't handle non-finite values.
Results may differ from a plain program's by a relative error of at most 0.015.
Values may be sent and summed in bfloat16 or wider, within the bound.
A program may use at most 256 MiB of HBM per device.

v0:
```python
import jax
import jax.numpy as jnp
from jax import lax
from jax.sharding import PartitionSpec as P

DIM = 512
HEADS = 16
HEAD_DIM = 32
WIN = 16
SHIFT = 8
CAP = 3


NORM_EPS = 1e-05


def entering(part, axis, combine, identity):
    place = lax.axis_index(axis)
    gathered = lax.all_gather(part, axis)
    state = jnp.zeros_like(part) + jnp.asarray(identity, part.dtype)

    def one(turn, state):
        return combine(state, lax.dynamic_index_in_dim(gathered, turn, 0, False))

    return lax.fori_loop(0, place, one, state)


def extended(block, sides, width):
    for axis, dim in sides:
        count = lax.axis_size(axis)
        forward = [(i, i + 1) for i in range(count - 1)]
        forward.append((count - 1, 0))
        backward = [(target, source) for source, target in forward]
        low = lax.ppermute(
            lax.slice_in_dim(block, block.shape[dim] - width, None, axis=dim), axis, forward
        )
        high = lax.ppermute(lax.slice_in_dim(block, 0, width, axis=dim), axis, backward)
        block = jnp.concatenate([low, block, high], axis=dim)
    return block


def layer_norm(values, norm_gain, norm_shift):
    average = jnp.mean(values, axis=-1, keepdims=True)
    centred = values - average
    variance = jnp.mean(centred * centred, axis=-1, keepdims=True)
    return centred * lax.rsqrt(variance + NORM_EPS) * norm_gain + norm_shift


def relative_bias(table):
    span = 2 * WIN - 1
    square = table.reshape(HEADS, span, span)
    inside = jnp.arange(WIN, dtype=jnp.int32)
    offsets = jnp.arange(span, dtype=jnp.int32)
    stepped = inside[:, None] - inside[None, :] + (WIN - 1)
    picker = (stepped[:, :, None] == offsets[None, None, :]).astype(jnp.float32)
    by_cols = jnp.einsum("hab,csb->hacs", square, picker, precision=lax.Precision.HIGHEST)
    full = jnp.einsum("pra,hacs->hpcrs", picker, by_cols, precision=lax.Precision.HIGHEST)
    return full.reshape(HEADS, WIN * WIN, WIN * WIN)


def to_windows(token_grid):
    rows_span, cols_span = (token_grid.shape[0], token_grid.shape[1])
    trailing = token_grid.shape[2:]
    blocked = token_grid.reshape((rows_span // WIN, WIN, cols_span // WIN, WIN) + trailing)
    axes_order = (0, 2, 1, 3) + tuple(range(4, 4 + len(trailing)))
    return blocked.transpose(axes_order).reshape(
        (rows_span // WIN * (cols_span // WIN), WIN * WIN) + trailing
    )


def from_windows(blocks, rows_span, cols_span):
    trailing = blocks.shape[2:]
    blocked = blocks.reshape((rows_span // WIN, cols_span // WIN, WIN, WIN) + trailing)
    axes_order = (0, 2, 1, 3) + tuple(range(4, 4 + len(trailing)))
    return blocked.transpose(axes_order).reshape((rows_span, cols_span) + trailing)


def wrap_labels(first_row, first_col, rows_span, cols_span, image_rows, image_cols):
    row_place = (first_row + jnp.arange(rows_span, dtype=jnp.int32)) % image_rows
    col_place = (first_col + jnp.arange(cols_span, dtype=jnp.int32)) % image_cols
    return (2 * (row_place < SHIFT).astype(jnp.int32))[:, None] + (col_place < SHIFT).astype(
        jnp.int32
    )[None, :]


def unit_rows(part):
    widened = part.astype(jnp.float32)
    length = jnp.sqrt(jnp.sum(widened * widened, axis=-1, keepdims=True))
    return (widened / jnp.maximum(length, 1.0)).astype(jnp.bfloat16)


def attention(blocks, labels, layer_id, params, pos_bias):
    w_qkv, b_qkv, w_proj, b_proj, w_up, b_up, w_down, b_down, norm_gain, norm_shift, logit_scale = (
        params
    )
    amount = blocks.shape[0]
    flat_rows = blocks.reshape(amount * WIN * WIN, DIM)
    packed = (
        jnp.dot(flat_rows, w_qkv[layer_id], preferred_element_type=jnp.float32) + b_qkv[layer_id]
    ).astype(jnp.bfloat16)
    packed = packed.reshape(amount, WIN * WIN, 3, HEADS, HEAD_DIM)
    queries = unit_rows(packed[:, :, 0])
    keyed = unit_rows(packed[:, :, 1])
    values = packed[:, :, 2]
    scores = jnp.einsum("nqhd,nkhd->nhqk", queries, keyed, preferred_element_type=jnp.float32)
    scores = scores * logit_scale[layer_id][None, :, None, None] + pos_bias[None]
    allowed = labels[:, None, :, None] == labels[:, None, None, :]
    raised = jnp.where(allowed, jnp.exp(scores), 0.0)
    weights = (raised / jnp.sum(raised, axis=-1, keepdims=True)).astype(jnp.bfloat16)
    context = jnp.einsum(
        "nhqk,nkhd->nqhd", weights, values, preferred_element_type=jnp.float32
    ).astype(jnp.bfloat16)
    attended = (
        jnp.dot(
            context.reshape(amount * WIN * WIN, DIM),
            w_proj[layer_id],
            preferred_element_type=jnp.float32,
        )
        + b_proj[layer_id]
    )
    return attended.reshape(amount, WIN * WIN, DIM)


def window_attention(blocks, labels, layer_id, params, position_table):
    pos_bias = relative_bias(position_table[layer_id])
    number = blocks.shape[0]
    group_size = 1
    for candidate in (4, 3, 2):
        if group_size == 1 and number % candidate == 0:
            group_size = candidate
    grouped = blocks.reshape(number // group_size, group_size, WIN * WIN, DIM)
    grouped_labels = labels.reshape(number // group_size, group_size, WIN * WIN)

    def per_group(item):
        return attention(item[0], item[1], layer_id, params, pos_bias)

    return lax.map(per_group, (grouped, grouped_labels)).reshape(number, WIN * WIN, DIM)


def token_part(base_rows, attended, layer_id, params):
    w_qkv, b_qkv, w_proj, b_proj, w_up, b_up, w_down, b_down, norm_gain, norm_shift, logit_scale = (
        params
    )
    middle = (
        base_rows.astype(jnp.float32)
        + layer_norm(attended, norm_gain[layer_id, 0], norm_shift[layer_id, 0])
    ).astype(jnp.bfloat16)
    expanded = jax.nn.gelu(
        jnp.dot(middle, w_up[layer_id], preferred_element_type=jnp.float32) + b_up[layer_id],
        approximate=False,
    ).astype(jnp.bfloat16)
    reduced = (
        jnp.dot(expanded, w_down[layer_id], preferred_element_type=jnp.float32) + b_down[layer_id]
    )
    return (
        middle.astype(jnp.float32)
        + layer_norm(reduced, norm_gain[layer_id, 1], norm_shift[layer_id, 1])
    ).astype(jnp.bfloat16)


def swin_block(blocks, labels, layer_id, params, position_table):
    number = blocks.shape[0]
    attended = window_attention(blocks, labels, layer_id, params, position_table).reshape(
        number * WIN * WIN, DIM
    )
    finished = token_part(blocks.reshape(number * WIN * WIN, DIM), attended, layer_id, params)
    return finished.reshape(blocks.shape)


def add_counts(earlier, later):
    return earlier + later


def move_clear(blocks, clear_flag, params, position_table):
    number = blocks.shape[0]
    group_cols = lax.axis_size("col")
    here_count = jnp.sum(clear_flag)
    before = entering(here_count, "col", add_counts, jnp.zeros((), jnp.int32))
    ranks = before + jnp.cumsum(clear_flag) - clear_flag
    owners = ranks % group_cols
    places = ranks // group_cols
    select = (owners[None, :] == jnp.arange(group_cols, dtype=jnp.int32)[:, None]) & (
        clear_flag[None, :] == 1
    )
    select_bf = select.astype(jnp.bfloat16)
    flat_blocks = blocks.reshape(number, WIN * WIN * DIM)
    outgoing = jnp.dot(select_bf, flat_blocks, preferred_element_type=jnp.float32).astype(
        jnp.bfloat16
    )
    slot_codes = jnp.where(
        jnp.any(select, axis=1), jnp.sum(select.astype(jnp.int32) * places[None, :], axis=1), -1
    ).astype(jnp.int32)
    arrived, arrived_codes = (
        lax.all_to_all(outgoing, "col", split_axis=0, concat_axis=0, tiled=True),
        lax.all_to_all(slot_codes, "col", split_axis=0, concat_axis=0, tiled=True),
    )
    pick = (arrived_codes[None, :] == jnp.arange(CAP, dtype=jnp.int32)[:, None]).astype(
        jnp.bfloat16
    )
    working = (
        jnp.dot(pick, arrived, preferred_element_type=jnp.float32)
        .astype(jnp.bfloat16)
        .reshape(CAP, WIN * WIN, DIM)
    )
    plain_labels = jnp.zeros((CAP, WIN * WIN), jnp.int32)
    processed = swin_block(working, plain_labels, 0, params, position_table)
    homeward = jnp.dot(
        pick.T, processed.reshape(CAP, WIN * WIN * DIM), preferred_element_type=jnp.float32
    ).astype(jnp.bfloat16)
    returned = lax.all_to_all(homeward, "col", split_axis=0, concat_axis=0, tiled=True)
    landed = (
        jnp.dot(select_bf.T, returned, preferred_element_type=jnp.float32)
        .astype(jnp.bfloat16)
        .reshape(blocks.shape)
    )
    return jnp.where((clear_flag == 1)[:, None, None], landed, blocks)


def body(
    tokens,
    cloud_mask,
    w_qkv,
    b_qkv,
    w_proj,
    b_proj,
    w_up,
    b_up,
    w_down,
    b_down,
    norm_gain,
    norm_shift,
    logit_scale,
    position_table,
):
    params = (
        w_qkv,
        b_qkv,
        w_proj,
        b_proj,
        w_up,
        b_up,
        w_down,
        b_down,
        norm_gain,
        norm_shift,
        logit_scale,
    )
    tile_rows, tile_cols = (tokens.shape[0], tokens.shape[1])
    blocks = to_windows(tokens)
    clear_flag = cloud_mask.reshape(-1)
    after_first = move_clear(blocks, clear_flag, params, position_table)
    token_grid = from_windows(after_first, tile_rows, tile_cols)
    image_rows = tile_rows * lax.axis_size("row")
    image_cols = tile_cols * lax.axis_size("col")
    top_row = lax.axis_index("row") * tile_rows
    left_col = lax.axis_index("col") * tile_cols
    padded = extended(token_grid, (("row", 0), ("col", 1)), SHIFT)
    rows_span = tile_rows + 2 * SHIFT
    cols_span = tile_cols + 2 * SHIFT
    labels = wrap_labels(
        top_row - SHIFT, left_col - SHIFT, rows_span, cols_span, image_rows, image_cols
    )
    attended = window_attention(to_windows(padded), to_windows(labels), 1, params, position_table)
    attended_grid = from_windows(attended, rows_span, cols_span)[
        SHIFT : SHIFT + tile_rows, SHIFT : SHIFT + tile_cols
    ]
    finished = token_part(
        token_grid.reshape(tile_rows * tile_cols, DIM),
        attended_grid.reshape(tile_rows * tile_cols, DIM),
        1,
        params,
    )
    return finished.reshape(tile_rows, tile_cols, DIM)


def solution(mesh):
    return jax.shard_map(
        body,
        mesh=mesh,
        in_specs=(
            P("row", "col", None),
            P("row", "col"),
            P(),
            P(),
            P(),
            P(),
            P(),
            P(),
            P(),
            P(),
            P(),
            P(),
            P(),
            P(),
        ),
        out_specs=P("row", "col", None),
        check_vma=False,
    )
```

profile of v0, /device:TPU:1, one launch (start us, length us, event | category | flops | bytes accessed | tf_op | source)
XLA Modules:
  0.0 586.3 jit_solution(3270752765887399047)
XLA Ops:
  5.4 14.5 %all-reduce = s32[16]{0:T(128)S(1)} all-reduce(s32[16]{0:T(128)S(1)} %dynamic-update-slice), channel_id=1, replica_groups=mesh['row'=8,'col'=16] {'col'}, use_global_device_ids=true, to_apply=%add | all-reduce | flops 16 | bytes 128
  21.0 19.0 %all-to-all-start = ((s32[16,1,1]{2,1,0:T(1,128)}), s32[16,1,1]{2,1,0:T(1,128)S(1)}, u32[]{:S(2)}, u32[]{:S(2)}) async-start(s32[16,1,1]{2,1,0:T(1,128)} %copy.138), calls=%async_computation | async-start | bytes 16384 | tf_op jit(solution)/shard_map/all_to_all | solution.py:195
  49.6 6.7 %reduce.8 = bf16[16,131072]{1,0:T(8,128)(2,1)} reduce(bf16[16,1,131072]{2,0,1:T(8,128)(2,1)} %fusion.16, bf16[]{:T(256)} %broadcast.443), dimensions={1}, to_apply=%copy.140.reduce_sub_computation | reduce | bytes 8388610 | tf_op jit(solution)/shard_map/all_to_all | solution.py:194
  56.3 6.7 %reshape.403 = bf16[16,2,65536]{2,1,0:T(2,128)(2,1)} reshape(bf16[16,131072]{1,0:T(8,128)(2,1)} %reduce.8) | data formatting | bytes 8388608
  63.0 7.2 %all-to-all-start.1 = ((bf16[16,2,65536]{2,1,0:T(2,128)(2,1)}), bf16[16,2,65536]{2,1,0:T(2,128)(2,1)}, u32[]{:S(2)}, u32[]{:S(2)}) async-start(bf16[16,2,65536]{2,1,0:T(2,128)(2,1)} %reshape.403), calls=%async_computation.1 | async-start | bytes 8388608 | tf_op jit(solution)/shard_map/all_to_all | solution.py:194
  71.6 17.4 %convolution_bitcast_fusion.1 = f32[16,16,16,16,16]{3,4,1,2,0:T(8,128)} fusion(f32[16,16,16,31]{3,1,0,2:T(8,128)S(1)} %fusion.84, s32[16,16]{1,0:T(8,128)S(1)} %subtract_add_fusion), kind=kOutput, calls=%fused_computation.43 | convolution fusion | flops 390078208 | bytes 4703232 | tf_op jit(solution)/shard_map/pra,hacs->hpcrs/dot_general | solution.py:57
  89.0 41.4 %copy.167 = f32[16,16,16,16,16]{2,1,4,3,0:T(8,128)} copy(f32[16,16,16,16,16]{3,4,1,2,0:T(8,128)} %convolution_bitcast_fusion.1) | data formatting | bytes 8388608 | tf_op jit(solution)/shard_map/while/body/eval_jaxpr/add | solution.py:106
  130.4 23.5 %reshape.396 = f32[16,256,256]{1,2,0:T(8,128)} reshape(f32[16,16,16,16,16]{2,1,4,3,0:T(8,128)} %copy.167) | data formatting | bytes 8388608 | tf_op jit(solution)/shard_map/while/body/eval_jaxpr/add | solution.py:106
  156.8 12.5 %reshape.404 = bf16[16,1,131072]{2,1,0:T(2,128)(2,1)} reshape(bf16[16,2,65536]{2,1,0:T(2,128)(2,1)} %all-to-all-done.1) | data formatting | bytes 8388608
  169.3 8.1 %convolution_convert_fusion.3 = bf16[3,131072]{1,0:T(4,128)(2,1)S(1)} fusion(bf16[16,1,131072]{2,1,0:T(2,128)(2,1)} %reshape.404, s32[16]{0:T(128)S(1)} %reduce.4), kind=kOutput, calls=%fused_computation.40 | convolution fusion | flops 12976176 | bytes 4980800 | tf_op jit(solution)/shard_map/dot_general | solution.py:201
  207.6 19.2 %fusion.181 = (f32[768]{0:T(1024)S(1)}, f32[768,512]{0,1:T(8,128)S(1)}) fusion(f32[512]{0:T(512)S(1)} %bitcast.311, bf16[2,2048,512]{2,1,0:T(8,128)(2,1)} %param.26, bf16[768,512]{0,1:T(8,128)(2,1)S(1)} %add_convert_fusion.5, f32[2048]{0:T(1024)S(1)} %bitcast.309, bf16[2,512,2048]{2,1,0:T(8,128)(2,1)} %param.24), kind=kOutput, calls=%fused_computation.270 | convolution fusion | flops 3325820160 | bytes 6566912 | tf_op jit(solution)/shard_map/dot_general | solution.py:153
  231.2 6.7 %reduce.9 = bf16[16,131072]{1,0:T(8,128)(2,1)} reduce(bf16[16,1,131072]{2,0,1:T(8,128)(2,1)} %fusion.17, bf16[]{:T(256)} %broadcast.443), dimensions={1}, to_apply=%copy.151.reduce_sub_computation | reduce | bytes 8388610 | tf_op jit(solution)/shard_map/all_to_all | solution.py:210
  237.9 6.8 %reshape.405 = bf16[16,2,65536]{2,1,0:T(2,128)(2,1)} reshape(bf16[16,131072]{1,0:T(8,128)(2,1)} %reduce.9) | data formatting | bytes 8388608
  244.7 6.9 %all-to-all-start.2 = ((bf16[16,2,65536]{2,1,0:T(2,128)(2,1)}), bf16[16,2,65536]{2,1,0:T(2,128)(2,1)}, u32[]{:S(2)}, u32[]{:S(2)}) async-start(bf16[16,2,65536]{2,1,0:T(2,128)(2,1)} %reshape.405), calls=%async_computation.2 | async-start | bytes 8388608 | tf_op jit(solution)/shard_map/all_to_all | solution.py:210
  254.3 46.3 %all-to-all-done.2 = bf16[16,2,65536]{2,1,0:T(2,128)(2,1)} async-done(((bf16[16,2,65536]{2,1,0:T(2,128)(2,1)}), bf16[16,2,65536]{2,1,0:T(2,128)(2,1)}, u32[]{:S(2)}, u32[]{:S(2)}) %all-to-all-start.2) | async-done | bytes 4194336 | tf_op jit(solution)/shard_map/all_to_all | solution.py:210
  300.6 12.3 %reshape.406 = bf16[16,1,131072]{2,1,0:T(2,128)(2,1)} reshape(bf16[16,2,65536]{2,1,0:T(2,128)(2,1)} %all-to-all-done.2) | data formatting | bytes 8388608
  312.9 8.1 %convolution_convert_fusion.2 = bf16[6,131072]{1,0:T(8,128)(2,1)S(1)} fusion(bf16[16,1,131072]{2,1,0:T(2,128)(2,1)} %reshape.406, s32[6]{0:T(128)S(1)} %and_select_fusion.1, pred[6]{0:T(512)(128)(4,1)S(1)} %broadcast_compare_fusion.2), kind=kOutput, calls=%fused_computation.39 | convolution fusion | flops 25952448 | bytes 5767198 | tf_op jit(solution)/shard_map/dot_general | solution.py:212
  323.6 6.0 %collective-permute-start = (bf16[8,48,512]{2,1,0:T(8,128)(2,1)S(1)}, bf16[8,48,512]{2,1,0:T(8,128)(2,1)S(1)}, u32[]{:S(2)}, u32[]{:S(2)}) collective-permute-start(bf16[8,48,512]{2,1,0:T(8,128)(2,1)S(1)} %get-tuple-element.217), channel_id=1, source_target_pairs={{0,16},{16,32},{32,48},{48,64},{64,80},{80,96},{96,112},{112,0},{1... | collective-permute-start | bytes 1179656 | tf_op jit(solution)/shard_map/ppermute | solution.py:34
  329.6 17.3 %convolution_bitcast_fusion = f32[16,16,16,16,16]{3,4,1,2,0:T(8,128)} fusion(f32[16,16,16,31]{3,1,0,2:T(8,128)S(1)} %copy-done.7, s32[16,16]{1,0:T(8,128)S(1)} %subtract_add_fusion), kind=kOutput, calls=%fused_computation.42 | convolution fusion | flops 390078208 | bytes 4703232 | tf_op jit(solution)/shard_map/pra,hacs->hpcrs/dot_general | solution.py:57
  352.8 41.5 %copy.154 = f32[16,16,16,16,16]{2,1,4,3,0:T(8,128)} copy(f32[16,16,16,16,16]{3,4,1,2,0:T(8,128)} %convolution_bitcast_fusion) | data formatting | bytes 8388608 | tf_op jit(solution)/shard_map/while | solution.py:137
  394.2 23.5 %add.550 = f32[16,256,256]{1,2,0:T(8,128)} reshape(f32[16,16,16,16,16]{2,1,4,3,0:T(8,128)} %copy.154) | data formatting | bytes 8388608 | tf_op jit(solution)/shard_map/while/body/eval_jaxpr/add | solution.py:106
  422.1 112.8 %while.26 = (s32[]{:T(128)}, f32[3,4,256,512]{3,2,1,0:T(8,128)}, bf16[3,4,256,512]{3,2,1,0:T(8,128)(2,1)S(1)}, bf16[2,512,1536]{2,1,0:T(8,128)(2,1)}, f32[2,1536...) while((s32[]{:T(128)}, f32[3,4,256,512]{3,2,1,0:T(8,128)}, ...), condition=%wide.wide.region_17.18_spmd, body=%wide.wide.region_13.17_spmd.sunk | while | flops 2732834816 | bytes 134649360 | solution.py:137
  430.4 4.8 reshape.409
  438.7 9.0 %fusion.217 = (f32[4,16,256]{2,1,0:T(8,128)S(1)}, f32[4,16,256,256]{2,3,1,0:T(8,128)}) fusion(f32[16,256,256]{1,2,0:T(8,128)S(1)} %copy-done, f32[16]{0:T(128)S(1)} %slice_bitcast_fusion.8, pred[4,256,256]{1,2,0:T(8,128)(4,1)S(1)} %broadcast_compare_fusion.5, bf16[4,256,16,32]{1,0,3,2:T(4,128)(2,1)S(1)} %get-tuple-element.396, ...), kind=kOutput, calls=%fused_computation.2.clone.clone.1 | convolution fusion | flops 285196288 | bytes 23396416 | tf_op jit(solution)/shard_map/while/body/eval_jaxpr/nqhd,nkhd->nhqk/dot_general | solution.py:105
  448.1 8.5 %fusion.218 = bf16[4,256,16,32]{1,3,2,0:T(8,128)(2,1)S(1)} fusion(f32[4,16,256,256]{2,3,1,0:T(8,128)} %get-tuple-element.398, f32[4,16,256]{2,1,0:T(8,128)S(1)} %get-tuple-element.399, f32[16,256,256]{1,2,0:T(8,128)S(1)} %copy-done, f32[16]{0:T(128)S(1)} %slice_bitcast_fusion.8, pred[4,256,256]{1,2,0:T(8,128)(4,1)S(1)} %broadcast_compare_fusion.5, ...), kind=kOutput, calls=%fused_computation.17.clone.clone.1 | convolution fusion | flops 289931264 | bytes 23396416 | tf_op jit(solution)/shard_map/while/body/eval_jaxpr/nhqk,nkhd->nqhd/dot_general | solution.py:110
  467.8 4.8 reshape.409
  476.2 9.0 %fusion.217 = (f32[4,16,256]{2,1,0:T(8,128)S(1)}, f32[4,16,256,256]{2,3,1,0:T(8,128)}) fusion(f32[16,256,256]{1,2,0:T(8,128)S(1)} %copy-done, f32[16]{0:T(128)S(1)} %slice_bitcast_fusion.8, pred[4,256,256]{1,2,0:T(8,128)(4,1)S(1)} %broadcast_compare_fusion.5, bf16[4,256,16,32]{1,0,3,2:T(4,128)(2,1)S(1)} %get-tuple-element.396, ...), kind=kOutput, calls=%fused_computation.2.clone.clone.1 | convolution fusion | flops 285196288 | bytes 23396416 | tf_op jit(solution)/shard_map/while/body/eval_jaxpr/nqhd,nkhd->nhqk/dot_general | solution.py:105
  485.6 8.5 %fusion.218 = bf16[4,256,16,32]{1,3,2,0:T(8,128)(2,1)S(1)} fusion(f32[4,16,256,256]{2,3,1,0:T(8,128)} %get-tuple-element.398, f32[4,16,256]{2,1,0:T(8,128)S(1)} %get-tuple-element.399, f32[16,256,256]{1,2,0:T(8,128)S(1)} %copy-done, f32[16]{0:T(128)S(1)} %slice_bitcast_fusion.8, pred[4,256,256]{1,2,0:T(8,128)(4,1)S(1)} %broadcast_compare_fusion.5, ...), kind=kOutput, calls=%fused_computation.17.clone.clone.1 | convolution fusion | flops 289931264 | bytes 23396416 | tf_op jit(solution)/shard_map/while/body/eval_jaxpr/nhqk,nkhd->nqhd/dot_general | solution.py:110
  505.3 4.8 reshape.409
  513.7 9.0 %fusion.217 = (f32[4,16,256]{2,1,0:T(8,128)S(1)}, f32[4,16,256,256]{2,3,1,0:T(8,128)}) fusion(f32[16,256,256]{1,2,0:T(8,128)S(1)} %copy-done, f32[16]{0:T(128)S(1)} %slice_bitcast_fusion.8, pred[4,256,256]{1,2,0:T(8,128)(4,1)S(1)} %broadcast_compare_fusion.5, bf16[4,256,16,32]{1,0,3,2:T(4,128)(2,1)S(1)} %get-tuple-element.396, ...), kind=kOutput, calls=%fused_computation.2.clone.clone.1 | convolution fusion | flops 285196288 | bytes 23396416 | tf_op jit(solution)/shard_map/while/body/eval_jaxpr/nqhd,nkhd->nhqk/dot_general | solution.py:105
  523.1 8.5 %fusion.218 = bf16[4,256,16,32]{1,3,2,0:T(8,128)(2,1)S(1)} fusion(f32[4,16,256,256]{2,3,1,0:T(8,128)} %get-tuple-element.398, f32[4,16,256]{2,1,0:T(8,128)S(1)} %get-tuple-element.399, f32[16,256,256]{1,2,0:T(8,128)S(1)} %copy-done, f32[16]{0:T(128)S(1)} %slice_bitcast_fusion.8, pred[4,256,256]{1,2,0:T(8,128)(4,1)S(1)} %broadcast_compare_fusion.5, ...), kind=kOutput, calls=%fused_computation.17.clone.clone.1 | convolution fusion | flops 289931264 | bytes 23396416 | tf_op jit(solution)/shard_map/while/body/eval_jaxpr/nhqk,nkhd->nqhd/dot_general | solution.py:110
  544.6 34.5 %fusion.184 = (f32[1536]{0:T(1024)S(1)}, f32[1536,512]{1,0:T(8,128)}) fusion(f32[512]{0:T(512)S(1)} %bitcast.310, bf16[2,2048,512]{2,1,0:T(8,128)(2,1)} %param.26, bf16[1536,512]{1,0:T(8,128)(2,1)} %bitcast.294, f32[2048]{0:T(1024)S(1)} %bitcast.308, bf16[2,512,2048]{2,1,0:T(8,128)(2,1)} %param.24), kind=kOutput, calls=%fused_computation.271 | convolution fusion | flops 6651640320 | bytes 8929280 | tf_op jit(solution)/shard_map/dot_general | solution.py:153
  (227 shorter events, 131.7 us)
Async XLA Ops:
  21.0 42.0 %all-to-all-start = ((s32[16,1,1]{2,1,0:T(1,128)}), s32[16,1,1]{2,1,0:T(1,128)S(1)}, u32[]{:S(2)}, u32[]{:S(2)}) async-start(s32[16,1,1]{2,1,0:T(1,128)} %copy.138), calls=%async_computation | async-start | bytes 16384 | tf_op jit(solution)/shard_map/all_to_all | solution.py:195
  56.3 13.9 %copy-start.12 = (f32[2,16,961]{2,1,0:T(8,128)S(1)}, f32[2,16,961]{2,1,0:T(8,128)}, u32[]{:S(2)}) copy-start(f32[2,16,961]{2,1,0:T(8,128)} %param.31) | copy-start | bytes 369028
  63.0 93.8 %all-to-all-start.1 = ((bf16[16,2,65536]{2,1,0:T(2,128)(2,1)}), bf16[16,2,65536]{2,1,0:T(2,128)(2,1)}, u32[]{:S(2)}, u32[]{:S(2)}) async-start(bf16[16,2,65536]{2,1,0:T(2,128)(2,1)} %reshape.403), calls=%async_computation.1 | async-start | bytes 8388608 | tf_op jit(solution)/shard_map/all_to_all | solution.py:194
  130.4 23.6 %copy-start.13 = (f32[2,1536]{1,0:T(2,128)S(1)}, f32[2,1536]{1,0:T(2,128)}, u32[]{:S(2)}) copy-start(f32[2,1536]{1,0:T(2,128)} %param.21) | copy-start | bytes 36868
  130.4 23.6 %copy-start.29 = (f32[2,16]{1,0:T(2,128)S(1)}, f32[2,16]{1,0:T(2,128)}, u32[]{:S(2)}) copy-start(f32[2,16]{1,0:T(2,128)} %param.30) | copy-start | bytes 388
  130.4 23.6 %copy-start.24 = (f32[2,512]{1,0:T(2,128)S(1)}, f32[2,512]{1,0:T(2,128)}, u32[]{:S(2)}) copy-start(f32[2,512]{1,0:T(2,128)} %param.27) | copy-start | bytes 12292
  130.4 24.2 %copy-start.21 = (f32[2,2,512]{2,1,0:T(2,128)S(1)}, f32[2,2,512]{2,1,0:T(2,128)}, u32[]{:S(2)}) copy-start(f32[2,2,512]{2,1,0:T(2,128)} %param.28) | copy-start | bytes 24580
  130.4 24.8 %copy-start.22 = (f32[2,2,512]{2,1,0:T(2,128)S(1)}, f32[2,2,512]{2,1,0:T(2,128)}, u32[]{:S(2)}) copy-start(f32[2,2,512]{2,1,0:T(2,128)} %param.29) | copy-start | bytes 24580
  130.4 25.4 %copy-start.18 = (f32[2,2048]{1,0:T(2,128)S(1)}, f32[2,2048]{1,0:T(2,128)}, u32[]{:S(2)}) copy-start(f32[2,2048]{1,0:T(2,128)} %param.25) | copy-start | bytes 49156
  178.5 4.5 copy-start.9
  202.5 3.9 slice-start
  202.5 3.9 copy-start.27
  244.7 7.2 %copy-start.26 = (s32[2,3]{1,0:T(2,128)S(1)}, s32[2,3]{1,0:T(2,128)}, u32[]{:S(2)}) copy-start(s32[2,3]{1,0:T(2,128)} %param.19) | copy-start | bytes 76
  244.7 55.9 %all-to-all-start.2 = ((bf16[16,2,65536]{2,1,0:T(2,128)(2,1)}), bf16[16,2,65536]{2,1,0:T(2,128)(2,1)}, u32[]{:S(2)}, u32[]{:S(2)}) async-start(bf16[16,2,65536]{2,1,0:T(2,128)(2,1)} %reshape.405), calls=%async_computation.2 | async-start | bytes 8388608 | tf_op jit(solution)/shard_map/all_to_all | solution.py:210
  312.9 8.6 %copy-start.8 = (bf16[32,48,512]{2,1,0:T(8,128)(2,1)S(1)}, bf16[32,48,512]{2,1,0:T(8,128)(2,1)}, u32[]{:S(2)}) copy-start(bf16[32,48,512]{2,1,0:T(8,128)(2,1)} %param.18) | copy-start | bytes 4718596
  321.0 8.6 %copy-start.7 = (f32[16,16,16,31]{3,1,0,2:T(8,128)S(1)}, f32[16,16,16,31]{3,1,0,2:T(8,128)}, u32[]{:S(2)}) copy-start(f32[16,16,16,31]{3,1,0,2:T(8,128)} %fusion.82) | copy-start | bytes 1523716
  323.6 97.7 %copy-start.2 = (bf16[2,3,16,16,512]{4,3,1,2,0:T(8,128)(2,1)}, bf16[2,3,16,16,512]{4,3,1,2,0:T(8,128)(2,1)S(1)}, u32[]{:S(2)}) copy-start(bf16[2,3,16,16,512]{4,3,1,2,0:T(8,128)(2,1)S(1)} %get-tuple-element.202) | copy-start | bytes 4718596
  323.6 23.3 %collective-permute-start = (bf16[8,48,512]{2,1,0:T(8,128)(2,1)S(1)}, bf16[8,48,512]{2,1,0:T(8,128)(2,1)S(1)}, u32[]{:S(2)}, u32[]{:S(2)}) collective-permute-start(bf16[8,48,512]{2,1,0:T(8,128)(2,1)S(1)} %get-tuple-element.217), channel_id=1, source_target_pairs={{0,16},{16,32},{32,48},{48,64},{64,80},{80,96},{96,112},{112,0},{1... | collective-permute-start | bytes 1179656 | tf_op jit(solution)/shard_map/ppermute | solution.py:34
  329.6 17.4 %collective-permute-start.1 = (bf16[8,48,512]{2,1,0:T(8,128)(2,1)S(1)}, bf16[8,48,512]{2,1,0:T(8,128)(2,1)S(1)}, u32[]{:S(2)}, u32[]{:S(2)}) collective-permute-start(bf16[8,48,512]{2,1,0:T(8,128)(2,1)S(1)} %get-tuple-element.218), channel_id=1, source_target_pairs={{16,0},{32,16},{48,32},{64,48},{80,64},{96,80},{112,96},{0,112},{1... | collective-permute-start | bytes 1179656 | tf_op jit(solution)/shard_map/ppermute | solution.py:37
  347.8 73.5 %collective-permute-start.2 = (bf16[48,8,512]{2,1,0:T(8,128)(2,1)}, bf16[48,8,512]{2,1,0:T(8,128)(2,1)S(1)}, u32[]{:S(2)}, u32[]{:S(2)}) collective-permute-start(bf16[48,8,512]{2,1,0:T(8,128)(2,1)} %get-tuple-element.215), channel_id=1, source_target_pairs={{0,1},{1,2},{2,3},{3,4},{4,5},{5,6},{6,7},{7,8},{8,9},{9,10},{10,1... | collective-permute-start | bytes 1179656 | tf_op jit(solution)/shard_map/ppermute | solution.py:34
  348.1 73.1 %collective-permute-start.3 = (bf16[48,8,512]{2,1,0:T(8,128)(2,1)S(1)}, bf16[48,8,512]{2,1,0:T(8,128)(2,1)S(1)}, u32[]{:S(2)}, u32[]{:S(2)}) collective-permute-start(bf16[48,8,512]{2,1,0:T(8,128)(2,1)S(1)} %get-tuple-element.216), channel_id=1, source_target_pairs={{1,0},{2,1},{3,2},{4,3},{5,4},{6,5},{7,6},{8,7},{9,8},{10,9},{11,1... | collective-permute-start | bytes 1179656 | tf_op jit(solution)/shard_map/ppermute | solution.py:37
  430.4 8.3 %copy-start.30 = (f32[2,16]{1,0:T(2,128)S(1)}, f32[2,16]{1,0:T(2,128)}, u32[]{:S(2)}) copy-start(f32[2,16]{1,0:T(2,128)} %get-tuple-element.451) | copy-start | bytes 388 | tf_op jit(solution)/shard_map/while
  448.1 9.6 %copy-start.28 = (bf16[2,512,512]{2,1,0:T(8,128)(2,1)S(1)}, bf16[2,512,512]{2,1,0:T(8,128)(2,1)}, u32[]{:S(2)}) copy-start(bf16[2,512,512]{2,1,0:T(8,128)(2,1)} %get-tuple-element.453) | copy-start | bytes 3145732 | tf_op jit(solution)/shard_map/while
  467.8 8.3 %copy-start.30 = (f32[2,16]{1,0:T(2,128)S(1)}, f32[2,16]{1,0:T(2,128)}, u32[]{:S(2)}) copy-start(f32[2,16]{1,0:T(2,128)} %get-tuple-element.451) | copy-start | bytes 388 | tf_op jit(solution)/shard_map/while
  485.6 9.6 %copy-start.28 = (bf16[2,512,512]{2,1,0:T(8,128)(2,1)S(1)}, bf16[2,512,512]{2,1,0:T(8,128)(2,1)}, u32[]{:S(2)}) copy-start(bf16[2,512,512]{2,1,0:T(8,128)(2,1)} %get-tuple-element.453) | copy-start | bytes 3145732 | tf_op jit(solution)/shard_map/while
  505.3 8.3 %copy-start.30 = (f32[2,16]{1,0:T(2,128)S(1)}, f32[2,16]{1,0:T(2,128)}, u32[]{:S(2)}) copy-start(f32[2,16]{1,0:T(2,128)} %get-tuple-element.451) | copy-start | bytes 388 | tf_op jit(solution)/shard_map/while
  523.1 9.6 %copy-start.28 = (bf16[2,512,512]{2,1,0:T(8,128)(2,1)S(1)}, bf16[2,512,512]{2,1,0:T(8,128)(2,1)}, u32[]{:S(2)}) copy-start(bf16[2,512,512]{2,1,0:T(8,128)(2,1)} %get-tuple-element.453) | copy-start | bytes 3145732 | tf_op jit(solution)/shard_map/while
  538.8 5.8 copy-start.23
  538.8 5.8 copy-start.25
  544.6 36.9 %copy-start.4 = (f32[32,48,512]{2,1,0:T(8,128)S(1)}, f32[32,48,512]{2,1,0:T(8,128)}, u32[]{:S(2)}) copy-start(f32[32,48,512]{2,1,0:T(8,128)} %get-tuple-element.212) | copy-start | bytes 9437188
  544.6 36.9 %copy-start.19 = (f32[1,1,512]{2,1,0:T(1,128)S(1)}, f32[1,1,512]{2,1,0:T(1,128)}, u32[]{:S(2)}) copy-start(f32[1,1,512]{2,1,0:T(1,128)} %get-tuple-element.223) | copy-start | bytes 6148
  544.6 36.9 %copy-start.20 = (f32[1,1,512]{2,1,0:T(1,128)S(1)}, f32[1,1,512]{2,1,0:T(1,128)}, u32[]{:S(2)}) copy-start(f32[1,1,512]{2,1,0:T(1,128)} %get-tuple-element.227) | copy-start | bytes 6148
  (17 other events, 43.8 us)
where the time goes:
time: 597 us; the launch traced here: 586 us
  local copies, waits for them, and re-layouts  246 us (41%)
  matrix products  190 us (32%)
  waiting for transfers between devices  46.3 us (8%)
  starting transfers between devices  44.1 us (7%)
  other arithmetic  43.8 us (7%)
  blocking collectives  14.5 us (2%)
    add x3, local copies, waits for them, and re-layouts, attention(): scores * logit_scale[layer_id][None, :, None, None] + pos_bias[None]  88.5 us
    dot_general x2, matrix products, token_part(): jnp.dot(expanded, w_down[layer_id], preferred_element_type=jnp.float32)  53.6 us
    all_to_all x1, waiting for transfers between devices, move_clear(): lax.all_to_all(homeward, 'col', split_axis=0, concat_axis=0, tiled=True)  46.3 us
    unnamed x61, local copies, waits for them, and re-layouts  42.7 us
    while x1, local copies, waits for them, and re-layouts, window_attention(): lax.map(per_group, (grouped, grouped_labels))  41.5 us
    dot_general x2, matrix products, relative_bias(): jnp.einsum('pra,hacs->hpcrs', picker, by_cols, precision=lax.Precision.HI...  34.7 us
    dot_general x4, matrix products, attention(): jnp.einsum('nqhd,nkhd->nhqk', queries, keyed, preferred_element_type=jnp....  30.6 us
    dot_general x4, matrix products, attention(): jnp.einsum('nhqk,nkhd->nqhd', weights, values, preferred_element_type=jnp...  28.4 us
  transfers between devices with their start and end apart: 7, of which 1 were waited for; matrix products, arithmetic and copies ran while one was open for 34% of the time, Pallas kernels for 0%

commit v1 on v0

v1 whole, which is shorter than its diff:
```python
import functools

import jax
import jax.numpy as jnp
from jax import lax
from jax.experimental import pallas as pl
from jax.experimental.pallas import tpu as pltpu
from jax.sharding import PartitionSpec as P

DIM = 512
HEADS = 16
HEAD_DIM = 32
FF = 2048
WIN = 16
HALF = 8
SPAN = 31
POS = 961
TOK = WIN * WIN
NORM_EPS = 1e-05
LOG2E = 1.4426950408889634
LANES_POS = 1024

GELU_POLY = (
    0.7978842161310574,
    0.03633428346473718,
    -3.312995621886861e-05,
    -5.52401697057975e-05,
    3.969110988768427e-06,
    -1.3344650342438986e-07,
    1.8056185099931046e-09,
)
GELU_CAP = 32.0

F32 = jnp.float32
BF16 = jnp.bfloat16
MESH = pl.DeviceIdType.MESH


def dot(a, b):
    return jnp.dot(a, b, preferred_element_type=F32)


def gelu(x):
    u = jnp.minimum(x * x, GELU_CAP)
    p = GELU_POLY[-1]
    for c in GELU_POLY[-2::-1]:
        p = p * u + c
    h = 0.5 * x
    return h * jnp.tanh(x * p) + h


def layer_norm(v, g, s):
    m = jnp.mean(v, axis=-1, keepdims=True)
    c = v - m
    var = jnp.mean(c * c, axis=-1, keepdims=True)
    return c * lax.rsqrt(var + NORM_EPS) * g + s


def build_bias(table, tscr, wscr, bias):
    tscr[...] = jnp.zeros_like(tscr)
    for b in range(2):
        tscr[b * HEADS : (b + 1) * HEADS, 0:POS] = table[b] * LOG2E
    rows = lax.broadcasted_iota(jnp.int32, (LANES_POS, 256), 0)
    lane = lax.broadcasted_iota(jnp.int32, (1, 256), 1)
    target = (30 - (lane >> 3)) * SPAN + 7 - (lane & 7)
    pick = jnp.where(rows == target, 1.0, 0.0).astype(BF16)
    for d in range(3):
        t = tscr[...]
        rolled = [
            pltpu.roll(t, LANES_POS - (8 * d + c), 1) if 8 * d + c else t for c in range(8)
        ]
        r = jnp.concatenate(rolled, axis=0)
        hi = r.astype(BF16)
        r = r - hi.astype(F32)
        mid = r.astype(BF16)
        lo = (r - mid.astype(F32)).astype(BF16)
        w = dot(hi, pick) + dot(mid, pick) + dot(lo, pick)
        for half in range(2):
            wscr[half, d * 256 : (d + 1) * 256, :] = w[:, half * 128 : (half + 1) * 128]

    def expand(bh, carry):
        b = bh // HEADS
        h = bh % HEADS
        for d in range(3):
            rows8 = pl.ds(d * 256 + bh, 8, stride=32)
            w = jnp.concatenate([wscr[0, rows8, :], wscr[1, rows8, :]], axis=1)
            for rp in range(WIN):
                o = (15 - rp) * 8
                piece = w[:, o : o + 128]
                for bp in range(2):
                    bq = bp - (d - 1)
                    if 0 <= bq < 2:
                        bias[b, h, bp * 128 + rp * 8 : bp * 128 + rp * 8 + 8, bq * 128 : bq * 128 + 128] = piece
        return carry

    lax.fori_loop(0, 2 * HEADS, expand, 0)


def kernel(
    remote,
    tok_hbm, mask, wqkv_hbm, bqkv, wproj_hbm, bproj, wup_hbm, bup, wdown_hbm, bdown,
    gain, shift, lscale, table,
    out,
    tok, wqkv, wproj, wup, wdown, buf, bias, tscr, wscr, prob, vone, ctx, hid, same, load_sem, send_sem, recv_sem,
):
    tile_rows, tile_cols = tok.shape[0], tok.shape[1]
    wh, ww = tile_rows // WIN, tile_cols // WIN
    nwin = wh * ww
    own = tile_rows * HALF
    edge_rows = HALF * HALF
    halves = 2 * ww

    loads = [
        pltpu.make_async_copy(tok_hbm, tok, load_sem.at[0]),
        pltpu.make_async_copy(wqkv_hbm, wqkv, load_sem.at[1]),
        pltpu.make_async_copy(wproj_hbm, wproj, load_sem.at[2]),
        pltpu.make_async_copy(wup_hbm, wup, load_sem.at[3]),
        pltpu.make_async_copy(wdown_hbm, wdown, load_sem.at[4]),
    ]
    for c in loads:
        c.start()

    if remote:
        row, col = lax.axis_index("row"), lax.axis_index("col")
        nrow, ncol = lax.axis_size("row"), lax.axis_size("col")
        up, down = lax.rem(row + nrow - 1, nrow), lax.rem(row + 1, nrow)
        left, right = lax.rem(col + ncol - 1, ncol), lax.rem(col + 1, ncol)
        barrier = pltpu.get_barrier_semaphore()
        for dev in ((up, col), (row, left), (up, left), (down, col), (row, right), (down, right)):
            pl.semaphore_signal(barrier, inc=1, device_id=dev, device_id_type=MESH)
        pl.semaphore_wait(barrier, 6)
        last_row = row == nrow - 1
        last_col = col == ncol - 1

        def copy(k, src, dst, dev):
            return pltpu.make_async_remote_copy(
                src_ref=src, dst_ref=dst, send_sem=send_sem.at[k], recv_sem=recv_sem.at[k],
                device_id=dev, device_id_type=MESH,
            )

        first, second = buf.at[1], buf.at[2]
        inner = pl.ds(0, edge_rows)
        outer = pl.ds(own, edge_rows)
        halo = [
            copy(0, first.at[pl.ds(0, halves), inner], first.at[pl.ds(0, halves), outer], (up, col)),
            copy(1, first.at[0, pl.ds(0, own)], first.at[halves, pl.ds(0, own)], (row, left)),
            copy(2, first.at[0, inner], first.at[halves, outer], (up, left)),
        ]
        back = [[] for _ in range(nwin)]
        k = 3
        for i in range(wh):
            for j in range(ww):
                n = i * ww + j
                low, right_edge = i == wh - 1, j == ww - 1
                start = edge_rows + i * TOK // 2
                size = TOK // 2 - (edge_rows if low else 0)
                if low:
                    cnt = 1 if right_edge else 2
                    cols = pl.ds(2 * j + 1, cnt)
                    back[n].append(copy(k, second.at[cols, outer], second.at[cols, inner], (down, col)))
                    k += 1
                if right_edge:
                    rows = pl.ds(start, size)
                    back[n].append(copy(k, second.at[halves, rows], second.at[0, rows], (row, right)))
                    k += 1
                if low and right_edge:
                    back[n].append(copy(k, second.at[halves, outer], second.at[0, inner], (down, right)))
                    k += 1
    else:
        last_row = last_col = jnp.bool_(False)

    build_bias(table, tscr, wscr, bias)

    r256 = lax.broadcasted_iota(jnp.int32, (256, 256), 0)
    c256 = lax.broadcasted_iota(jnp.int32, (256, 256), 1)
    same[...] = jnp.where((r256 >> 5) == (c256 >> 5), 1.0, 0.0).astype(BF16)
    lane128 = lax.broadcasted_iota(jnp.int32, (TOK, 128), 1)
    for h in range(4):
        vone[h * TOK : (h + 1) * TOK, 128:256] = jnp.where((lane128 >> 5) == h, 1.0, 0.0).astype(BF16)

    loads[0].wait()
    for j in range(ww):
        t = tok[:, j * WIN : (j + 1) * WIN, :].astype(F32)
        for b in range(2):
            buf[0, 2 * j + b, 0:own, :] = t[:, b * HALF : (b + 1) * HALF, :].reshape(own, DIM).astype(BF16)
    for c in loads[1:]:
        c.wait()

    lane256 = lax.broadcasted_iota(jnp.int32, (TOK, 256), 1)
    lane512 = lax.broadcasted_iota(jnp.int32, (1, DIM), 1)

    def window(w, carry):
        b = w // nwin
        n = w % nwin
        idx = n + b * (nwin - 1 - 2 * n)
        i = idx // ww
        j = idx % ww
        if remote:
            @pl.when(w == nwin)
            def _():
                for c in halo:
                    c.wait_recv()

        cb = 2 * j + b
        r0 = pl.multiple_of(i * (TOK // 2) + b * edge_rows, edge_rows)
        half_rows = pl.ds(r0, TOK // 2)
        x = jnp.concatenate([buf[b, cb, half_rows, :], buf[b, cb + 1, half_rows, :]], axis=0)

        q = dot(x, wqkv[b, :, 0:DIM]) + bqkv[pl.ds(b, 1), 0:DIM]
        k_ = dot(x, wqkv[b, :, DIM : 2 * DIM]) + bqkv[pl.ds(b, 1), DIM : 2 * DIM]
        v = (dot(x, wqkv[b, :, 2 * DIM : 3 * DIM]) + bqkv[pl.ds(b, 1), 2 * DIM : 3 * DIM]).astype(BF16)
        sc = jnp.zeros((1, DIM), F32)
        for h in range(HEADS):
            sc = jnp.where((lane512 >> 5) == h, lscale[b, h] * LOG2E, sc)

        r2 = lax.broadcasted_iota(jnp.int32, (TOK, TOK), 0)
        c2 = lax.broadcasted_iota(jnp.int32, (TOK, TOK), 1)
        cut_row = jnp.logical_and(jnp.logical_and(last_row, b == 1), i == wh - 1)
        cut_col = jnp.logical_and(jnp.logical_and(last_col, b == 1), j == ww - 1)
        cut = cut_row.astype(jnp.int32) * edge_rows + cut_col.astype(jnp.int32) * (TOK // 2)
        allowed = jnp.where(((r2 ^ c2) & cut) == 0, 1.0, 0.0).astype(BF16)

        for g in range(2):
            lanes = slice(g * 256, (g + 1) * 256)
            qg, kg = q[:, lanes], k_[:, lanes]
            q2 = dot((qg * qg).astype(BF16), same[...])
            k2 = dot((kg * kg).astype(BF16), same[...])
            qn = (qg * lax.rsqrt(jnp.maximum(q2, 1.0)) * sc[:, lanes]).astype(BF16)
            kn = (kg * lax.rsqrt(jnp.maximum(k2, 1.0))).astype(BF16)
            for gg in range(2):
                v0 = g * 256 + gg * 128
                vg = v[:, v0 : v0 + 128]
                for h in range(4):
                    vone[h * TOK : (h + 1) * TOK, 0:128] = jnp.where(
                        (lane128 >> 5) == h, vg, jnp.zeros_like(vg)
                    )
                    hh = gg * 4 + h
                    qm = jnp.where((lane256 >> 5) == hh, qn, jnp.zeros_like(qn))
                    s = lax.dot_general(
                        qm, kn, (((1,), (1,)), ((), ())), preferred_element_type=F32
                    )
                    e = jnp.exp2(s + bias[b, g * 8 + hh]).astype(BF16) * allowed
                    prob[:, h * TOK : (h + 1) * TOK] = e
                o = dot(prob[...], vone[...])
                ctx[:, v0 : v0 + 128] = (o[:, 0:128] / o[:, 128:256]).astype(BF16)

        att = dot(ctx[...], wproj[b]) + bproj[pl.ds(b, 1), :]
        mid = x.astype(F32) + layer_norm(att, gain[b, 0:1, :], shift[b, 0:1, :])
        midb = mid.astype(BF16)
        for f in range(FF // 512):
            lanes = slice(f * 512, (f + 1) * 512)
            hid[:, lanes] = gelu(dot(midb, wup[b, :, lanes]) + bup[pl.ds(b, 1), lanes]).astype(BF16)
        red = dot(hid[...], wdown[b]) + bdown[pl.ds(b, 1), :]
        y = midb.astype(F32) + layer_norm(red, gain[b, 1:2, :], shift[b, 1:2, :])
        keep = jnp.logical_or(mask[i, j] == 1, b == 1)
        y = jnp.where(keep, y, x.astype(F32)).astype(BF16)
        buf[b + 1, cb, half_rows, :] = y[0 : TOK // 2]
        buf[b + 1, cb + 1, half_rows, :] = y[TOK // 2 :]

        if remote:
            @pl.when(w == ww)
            def _():
                for c in halo:
                    c.start()

            for n_ in range(nwin):
                if back[n_]:
                    @pl.when(w == 2 * nwin - 1 - n_)
                    def _(n_=n_):
                        for c in back[n_]:
                            c.start()
        return carry

    lax.fori_loop(0, 2 * nwin, window, 0)
    if remote:
        for c in halo:
            c.wait_send()
        for cs in back:
            for c in cs:
                c.wait()
    for j in range(ww):
        parts = [
            buf[2, 2 * j + b, 0:own, :].astype(F32).reshape(tile_rows, HALF, DIM) for b in range(2)
        ]
        out[:, j * WIN : (j + 1) * WIN, :] = jnp.concatenate(parts, axis=1).astype(BF16)


def body(remote, *args):
    tokens = args[0]
    tile_rows, tile_cols = tokens.shape[0], tokens.shape[1]
    ww = tile_cols // WIN
    vmem = pl.BlockSpec(memory_space=pltpu.VMEM)
    smem = pl.BlockSpec(memory_space=pltpu.SMEM)
    anym = pl.BlockSpec(memory_space=pl.ANY)
    return pl.pallas_call(
        functools.partial(kernel, remote),
        out_shape=jax.ShapeDtypeStruct(tokens.shape, BF16),
        in_specs=[anym, smem, anym, vmem, anym, vmem, anym, vmem, anym, vmem, vmem, vmem, smem, vmem],
        out_specs=vmem,
        scratch_shapes=[
            pltpu.VMEM(tokens.shape, BF16),
            pltpu.VMEM((2, DIM, 3 * DIM), BF16),
            pltpu.VMEM((2, DIM, DIM), BF16),
            pltpu.VMEM((2, DIM, FF), BF16),
            pltpu.VMEM((2, FF, DIM), BF16),
            pltpu.VMEM((3, 2 * ww + 1, (tile_rows + HALF) * HALF, DIM), BF16),
            pltpu.VMEM((2, HEADS, TOK, TOK), F32),
            pltpu.VMEM((2 * HEADS, LANES_POS), F32),
            pltpu.VMEM((2, 3 * 256, 128), F32),
            pltpu.VMEM((TOK, 4 * TOK), BF16),
            pltpu.VMEM((4 * TOK, 256), BF16),
            pltpu.VMEM((TOK, DIM), BF16),
            pltpu.VMEM((TOK, FF), BF16),
            pltpu.VMEM((256, 256), BF16),
            pltpu.SemaphoreType.DMA((5,)),
            pltpu.SemaphoreType.DMA((9,)),
            pltpu.SemaphoreType.DMA((9,)),
        ],
        compiler_params=pltpu.CompilerParams(
            collective_id=0 if remote else None,
            has_side_effects=remote,
            vmem_limit_bytes=56 * 1024 * 1024,
        ),
    )(*args)


def solution(mesh):
    return jax.shard_map(
        functools.partial(body, True),
        mesh=mesh,
        in_specs=(P("row", "col", None), P("row", "col")) + (P(),) * 12,
        out_specs=P("row", "col", None),
        check_vma=False,
    )
```

time: 597 us -> 86.4 us (0.14); the launches traced: 586 us -> 85.5 us
  local copies, waits for them, and re-layouts: 246 us -> 2.66 us
  matrix products: 190 us -> 0 us
  Pallas kernels: 0 us -> 82.8 us
  waiting for transfers between devices: 46.3 us -> 0 us
  starting transfers between devices: 44.1 us -> 0 us
  other arithmetic: 43.8 us -> 0 us
  blocking collectives: 14.5 us -> 0 us
    dot_general x26 -> x0, matrix products: 190 us -> none  [the longest x2 53.6 us: token_part(): jnp.dot(expanded, w_down[layer_id], preferred_element_type=jnp.float32)]
    add x7 -> x0, local copies, waits for them, and re-layouts: 91.4 us -> none  [the longest x3 88.5 us: attention(): scores * logit_scale[layer_id][None, :, None, None] + pos_bias[None]]
    pallas_call x0 -> x1, Pallas kernels: none -> 82.8 us  [body(): pl.pallas_call(functools.partial(kernel, remote), out_shape=jax.ShapeDtyp...]
    while x34 -> x0, local copies, waits for them, and re-layouts: 46.7 us -> none  [the longest x1 41.5 us: window_attention(): lax.map(per_group, (grouped, grouped_labels))]
    all_to_all x3 -> x0, waiting for transfers between devices: 46.3 us -> none  [the longest x1 46.3 us: move_clear(): lax.all_to_all(homeward, 'col', split_axis=0, concat_axis=0, tiled=True)]
    unnamed x61 -> x1, local copies, waits for them, and re-layouts: 42.7 us -> 2.66 us
    all_to_all x3 -> x0, starting transfers between devices: 33.1 us -> none  [the longest x1 19 us: move_clear(): lax.all_to_all(slot_codes, 'col', split_axis=0, concat_axis=0, tiled=True)]
    reshape x5 -> x0, local copies, waits for them, and re-layouts: 19.8 us -> none  [the longest x4 19 us: attention(): packed = packed.reshape(amount, WIN * WIN, 3, HEADS, HEAD_DIM)]
  transfers between devices with their start and end apart: 7 -> 0, of which waited for: 1 -> 0; matrix products, arithmetic and copies ran while one was open for 34% -> 0% of each run, Pallas kernels for 0% -> 0%
where the time goes in v1:
time: 86.4 us; the launch traced here: 85.5 us
  Pallas kernels  82.8 us (96%)
  local copies, waits for them, and re-layouts  2.66 us (3%)
    pallas_call x1, Pallas kernels, body(): pl.pallas_call(functools.partial(kernel, remote), out_shape=jax.ShapeDtyp...  82.8 us
    unnamed x1, local copies, waits for them, and re-layouts  2.66 us

profile of v1, /device:TPU:1, one launch (start us, length us, event | category | flops | bytes accessed | tf_op | source)
XLA Modules:
  0.0 85.5 jit_solution(10556007595975797108)
XLA Ops:
  0.0 82.8 %shard_map.136 = bf16[32,48,512]{2,1,0:T(8,128)(2,1)} custom-call(bf16[32,48,512]{2,1,0:T(8,128)(2,1)} %tok_hbm.1, s32[2,3]{1,0:T(2,128)} %mask.1, bf16[2,512,1536]{2,1,0:T(8,128)(2,1)} %wqkv_hbm.1, f32[2,1536]{1,0:T(2,128)} %bqkv.1, bf16[2,512,512]{2,1,0:T(8,128)(2,1)} %wproj_hbm.1, f32[2,512]{1,0:T(2,128)} %bproj.1, bf16[2,512,2048]{2,1,0:T(8,128)(2,1)} %wup_hbm.1, ...), custom_call_target="tpu_custom_call" | custom-call | tf_op jit(solution)/shard_map/pallas_call | solution.py:295
  82.8 2.7 %copy.16 = bf16[32,48,512]{2,1,0:T(8,128)(2,1)} copy(bf16[32,48,512]{2,1,0:T(8,128)(2,1)} %shard_map.136) | data formatting | bytes 3145728

commit v2 on v1

v2 whole, which is shorter than its diff:
```python
import functools

import jax
import jax.numpy as jnp
from jax import lax
from jax.experimental import pallas as pl
from jax.experimental.pallas import tpu as pltpu
from jax.sharding import PartitionSpec as P

DIM = 512
HEADS = 16
HEAD_DIM = 32
FF = 2048
WIN = 16
HALF = 8
SPAN = 31
POS = 961
TOK = WIN * WIN
NORM_EPS = 1e-05
LOG2E = 1.4426950408889634
LANES_POS = 1024
CHUNK = 256
ORDER = ((0, 1, 3, 2, 4, 5), (0, 3, 4, 5, 2, 1))
HALO_AFTER = 2
FIRST = [("start", 0)] + [(p, g) for g in range(2) for p in ("q", "k", "v", "unit")] + [("head", h) for h in range(16)]
LAST = [("merge", 0), ("norm", 0)] + [("widen", f) for f in range(8)] + [("narrow", 0), ("narrow", 1), ("finish", 0)]
OPENING = (
    ("start", 0), ("q", 0), ("k", 0), ("merge", 0), ("v", 0), ("unit", 0), ("norm", 0),
    ("q", 1), ("k", 1), ("v", 1),
)
AFTER = {
    0: [("widen", 0)], 1: [("unit", 1), ("widen", 1), ("widen", 2)], 2: [("widen", 3)], 3: [("widen", 4)],
    4: [("widen", 5), ("widen", 6)], 5: [("widen", 7), ("narrow", 0)], 6: [("narrow", 1)], 7: [("finish", 0)],
}


def mixed():
    steps = list(OPENING)
    for h in range(HEADS):
        steps += [("head", h)] + AFTER.get(h, [])
    return steps


MIXED = mixed()

GELU_POLY = (
    0.7978275766755302,
    0.036469930643555554,
    -0.00012547612359992849,
    -3.0467214006275725e-05,
    1.1126326266502673e-06,
)
PENALTY = -30000.0

F32 = jnp.float32
BF16 = jnp.bfloat16
MESH = pl.DeviceIdType.MESH


def dot(a, b):
    return jnp.dot(a, b, preferred_element_type=F32)


def twice_gelu(x):
    u = x * x
    p = GELU_POLY[-1]
    for c in GELU_POLY[-2::-1]:
        p = p * u + c
    return x * (jnp.tanh(x * p) + 1.0)


def layer_norm(v, g, s):
    m = jnp.mean(v, axis=-1, keepdims=True)
    c = v - m
    var = jnp.mean(c * c, axis=-1, keepdims=True)
    return c * lax.rsqrt(var + NORM_EPS) * g + s


def spread_table(table, tscr, wscr):
    tscr[...] = jnp.zeros_like(tscr)
    for b in range(2):
        tscr[b * HEADS : (b + 1) * HEADS, 0:POS] = table[b] * LOG2E
    t = tscr[...]
    r = jnp.concatenate([pltpu.roll(t, LANES_POS - c, 1) if c else t for c in range(8)], axis=0)
    hi = r.astype(BF16)
    lo = (r - hi.astype(F32)).astype(BF16)
    rows = lax.broadcasted_iota(jnp.int32, (LANES_POS, 256), 0)
    lane = lax.broadcasted_iota(jnp.int32, (1, 256), 1)
    target = (30 - (lane >> 3)) * SPAN + 7 - (lane & 7)
    for d in range(3):
        pick = jnp.where(rows == target + 8 * d, 1.0, 0.0).astype(BF16)
        w = dot(hi, pick) + dot(lo, pick)
        for half in range(2):
            wscr[half, d * 256 : (d + 1) * 256, :] = w[:, half * 128 : (half + 1) * 128]


def expand_bias(wscr, bias, b, h):
    lane = lax.broadcasted_iota(jnp.int32, (HALF, 128), 1)
    for d in range(3):
        rows8 = pl.ds(d * 256 + b * HEADS + h, 8, stride=32)
        w0, w1 = wscr[0, rows8, :], wscr[1, rows8, :]
        for rp in range(WIN):
            o = (15 - rp) * 8
            piece = pltpu.roll(jnp.where(lane < o, w1, w0), 128 - o, 1) if o else w0
            for bp in range(2):
                bq = bp - (d - 1)
                if 0 <= bq < 2:
                    bias[b, h, bp * 128 + rp * 8 : bp * 128 + rp * 8 + 8, bq * 128 : bq * 128 + 128] = piece


def kernel(
    remote,
    tok_hbm, mask, wqkv_hbm, bqkv, wproj_hbm, bproj, wup_hbm, bup, wdown_hbm, bdown,
    gain, shift, lscale, table,
    out,
    tok, wqkv, wproj, wup, wdown, buf, bias, tscr, wscr, prob, vone, ctx, hid, same, hmask, qlab, klab, load_sem, send_sem, recv_sem,
):
    tile_rows, tile_cols = tok.shape[0], tok.shape[1]
    wh, ww = tile_rows // WIN, tile_cols // WIN
    nwin = wh * ww
    own = tile_rows * HALF
    edge_rows = HALF * HALF
    halves = 2 * ww

    loads = [[pltpu.make_async_copy(tok_hbm, tok, load_sem.at[0])], []]
    for b in range(2):
        for k, (src, dst) in enumerate(((wqkv_hbm, wqkv), (wproj_hbm, wproj), (wup_hbm, wup), (wdown_hbm, wdown))):
            loads[b].append(pltpu.make_async_copy(src.at[b], dst.at[b], load_sem.at[1 + 4 * b + k]))
    for c in loads[0]:
        c.start()

    if remote:
        row, col = lax.axis_index("row"), lax.axis_index("col")
        nrow, ncol = lax.axis_size("row"), lax.axis_size("col")
        up, down = lax.rem(row + nrow - 1, nrow), lax.rem(row + 1, nrow)
        left, right = lax.rem(col + ncol - 1, ncol), lax.rem(col + 1, ncol)
        barrier = pltpu.get_barrier_semaphore()
        for dev in ((up, col), (row, left), (up, left), (down, col), (row, right), (down, right)):
            pl.semaphore_signal(barrier, inc=1, device_id=dev, device_id_type=MESH)
        pl.semaphore_wait(barrier, 6)
        last_row = row == nrow - 1
        last_col = col == ncol - 1

        def copy(k, src, dst, dev):
            return pltpu.make_async_remote_copy(
                src_ref=src, dst_ref=dst, send_sem=send_sem.at[k], recv_sem=recv_sem.at[k],
                device_id=dev, device_id_type=MESH,
            )

        first, second = buf.at[1], buf.at[2]
        inner = pl.ds(0, edge_rows)
        outer = pl.ds(own, edge_rows)
        halo = [
            copy(0, first.at[pl.ds(0, halves), inner], first.at[pl.ds(0, halves), outer], (up, col)),
            copy(1, first.at[0, pl.ds(0, own)], first.at[halves, pl.ds(0, own)], (row, left)),
            copy(2, first.at[0, inner], first.at[halves, outer], (up, left)),
        ]
        back = [[] for _ in range(nwin)]
        k = 3
        for i in range(wh):
            for j in range(ww):
                n = i * ww + j
                low, right_edge = i == wh - 1, j == ww - 1
                start = edge_rows + i * TOK // 2
                size = TOK // 2 - (edge_rows if low else 0)
                if low:
                    cnt = 1 if right_edge else 2
                    cols = pl.ds(2 * j + 1, cnt)
                    back[n].append(copy(k, second.at[cols, outer], second.at[cols, inner], (down, col)))
                    k += 1
                if right_edge:
                    rows = pl.ds(start, size)
                    back[n].append(copy(k, second.at[halves, rows], second.at[0, rows], (row, right)))
                    k += 1
                if low and right_edge:
                    back[n].append(copy(k, second.at[halves, outer], second.at[0, inner], (down, right)))
                    k += 1
    else:
        last_row = last_col = jnp.bool_(False)

    loads[0][0].wait()
    for j in range(ww):
        t = tok[:, j * WIN : (j + 1) * WIN, :].astype(F32)
        for b in range(2):
            buf[0, 2 * j + b, 0:own, :] = t[:, b * HALF : (b + 1) * HALF, :].reshape(own, DIM).astype(BF16)

    spread_table(table, tscr, wscr)

    r256 = lax.broadcasted_iota(jnp.int32, (256, 256), 0)
    c256 = lax.broadcasted_iota(jnp.int32, (256, 256), 1)
    same[...] = jnp.where((r256 >> 5) == (c256 >> 5), 1.0, 0.0).astype(BF16)
    head_lane = lax.broadcasted_iota(jnp.int32, (WIN, 128), 1) >> 5
    for h in range(4):
        hmask[h] = jnp.where(head_lane == h, 1.0, 0.0).astype(BF16)
    token = lax.broadcasted_iota(jnp.int32, (TOK, 128), 0)
    lane128 = lax.broadcasted_iota(jnp.int32, (TOK, 128), 1)
    for case in range(4):
        label = ((token >> 6) & 1) * (case & 2) + (token >> 7) * (case & 1)
        qlab[case] = jnp.where(lane128 == label, 1.0, 0.0).astype(BF16)
        klab[case] = jnp.where(jnp.logical_or(lane128 == label, lane128 > 3), 0.0, PENALTY).astype(BF16)
    for h in range(4):
        vone[h * TOK : (h + 1) * TOK, 128:256] = jnp.where((lane128 >> 5) == h, 1.0, 0.0).astype(BF16)
    lane512 = lax.broadcasted_iota(jnp.int32, (1, DIM), 1)

    def place(w):
        b = w // nwin
        n = w % nwin
        idx = jnp.int32(0)
        for k in range(nwin):
            idx = idx + jnp.where(n == k, jnp.where(b == 0, ORDER[0][k], ORDER[1][k]), 0)
        i = idx // ww
        j = idx % ww
        cb = 2 * j + b
        rows = pl.ds(pl.multiple_of(i * (TOK // 2) + b * edge_rows, edge_rows), TOK // 2)
        return b, i, j, cb, rows

    def load_x(b, cb, rows):
        return jnp.concatenate([buf[b, cb, rows, :], buf[b, cb + 1, rows, :]], axis=0)

    def attention(w):
        b, i, j, cb, rows = place(w)
        st = {}

        def start():
            st["x"] = load_x(b, cb, rows)
            sc = jnp.zeros((1, DIM), F32)
            for h in range(HEADS):
                sc = jnp.where((lane512 >> 5) == h, lscale[b, h] * LOG2E, sc)
            st["sc"] = sc
            cut_row = jnp.logical_and(jnp.logical_and(last_row, b == 1), i == wh - 1)
            cut_col = jnp.logical_and(jnp.logical_and(last_col, b == 1), j == ww - 1)
            st["case"] = cut_row.astype(jnp.int32) * 2 + cut_col.astype(jnp.int32)

        def project(part, g):
            lanes = slice(part * DIM + g * 256, part * DIM + (g + 1) * 256)
            r = dot(st["x"], wqkv[b, :, lanes]) + bqkv[pl.ds(b, 1), lanes]
            st[part, g] = r.astype(BF16) if part == 2 else r

        def unit(g):
            lanes = slice(g * 256, (g + 1) * 256)
            qg, kg = st[0, g], st[1, g]
            q2 = dot((qg * qg).astype(BF16), same[...])
            k2 = dot((kg * kg).astype(BF16), same[...])
            st["qn", g] = (qg * (lax.rsqrt(jnp.maximum(q2, 1.0)) * st["sc"][:, lanes])).astype(BF16)
            st["kn", g] = (kg * lax.rsqrt(jnp.maximum(k2, 1.0))).astype(BF16)

        def head(h):
            h4, g = h % 4, h // 8
            here = slice((h - h4) % 8 * HEAD_DIM, (h - h4) % 8 * HEAD_DIM + 128)
            only = hmask[h4][None]
            vg = st[2, g][:, here].reshape(WIN, WIN, 128)
            vone[h4 * TOK : (h4 + 1) * TOK, 0:128] = (vg * only).reshape(TOK, 128)
            qm = (st["qn", g][:, here].reshape(WIN, WIN, 128) * only).reshape(TOK, 128)
            s = lax.dot_general(
                jnp.concatenate([qm, qlab[st["case"]]], axis=1),
                jnp.concatenate([st["kn", g][:, here], klab[st["case"]]], axis=1),
                (((1,), (1,)), ((), ())), preferred_element_type=F32,
            )
            prob[:, h4 * TOK : (h4 + 1) * TOK] = jnp.exp2(s + bias[b, h]).astype(BF16)
            if h4 == 3:
                o = dot(prob[...], vone[...])
                v0 = (h - 3) * HEAD_DIM
                ctx[:, v0 : v0 + 128] = (o[:, 0:128] * pl.reciprocal(o[:, 128:256], approx=True)).astype(BF16)

        steps = {("start", 0): start}
        for g in range(2):
            steps["unit", g] = functools.partial(unit, g)
            for part in range(3):
                steps["qkv"[part], g] = functools.partial(project, part, g)
        for h in range(HEADS):
            steps["head", h] = functools.partial(head, h)
        return steps

    def feed(w):
        b, i, j, cb, rows = place(w)
        st = {}

        def merge():
            st["x"] = load_x(b, cb, rows).astype(F32)
            st["att"] = dot(ctx[...], wproj[b]) + bproj[pl.ds(b, 1), :]

        def norm():
            mid = st["x"] + layer_norm(st["att"], gain[b, 0:1, :], shift[b, 0:1, :])
            st["mid"] = mid.astype(BF16)

        def widen(f):
            lanes = slice(f * CHUNK, (f + 1) * CHUNK)
            up_ = dot(st["mid"], wup[b, :, lanes]) + bup[pl.ds(b, 1), lanes]
            hid[:, lanes] = twice_gelu(up_).astype(BF16)

        def narrow(n):
            lanes = slice(n * 256, (n + 1) * 256)
            st["red", n] = 0.5 * dot(hid[...], wdown[b, :, lanes]) + bdown[pl.ds(b, 1), lanes]

        def finish():
            y = st["mid"].astype(F32) + layer_norm(jnp.concatenate([st["red", 0], st["red", 1]], axis=1), gain[b, 1:2, :], shift[b, 1:2, :])
            keep = jnp.logical_or(mask[i, j] == 1, b == 1)
            y = jnp.where(keep, y, st["x"]).astype(BF16)
            buf[b + 1, cb, rows, :] = y[0 : TOK // 2]
            buf[b + 1, cb + 1, rows, :] = y[TOK // 2 :]

        steps = {("merge", 0): merge, ("norm", 0): norm, ("finish", 0): finish}
        for f in range(FF // CHUNK):
            steps["widen", f] = functools.partial(widen, f)
        for n in range(2):
            steps["narrow", n] = functools.partial(narrow, n)
        return steps

    for c in loads[0][1:]:
        c.wait()
    for c in loads[1]:
        c.start()
    first_steps = attention(jnp.int32(0))
    for step in FIRST:
        if step[0] == "head":
            for b in range(2):
                expand_bias(wscr, bias, b, step[1])
        first_steps[step]()

    def both(t, carry):
        @pl.when(t == nwin)
        def _():
            for c in loads[1]:
                c.wait()

        if remote:
            @pl.when(t == nwin + 1)
            def _():
                for c in halo:
                    c.wait_recv()

        steps = {**attention(t), **feed(t - 1)}
        for step in MIXED:
            steps[step]()

        if remote:
            for pos in range(nwin):
                if ORDER[0][pos] == HALO_AFTER:
                    @pl.when(t == pos + 1)
                    def _():
                        for c in halo:
                            c.start()
                n_ = ORDER[1][pos]
                if back[n_] and pos < nwin - 1:
                    @pl.when(t == nwin + pos + 1)
                    def _(n_=n_):
                        for c in back[n_]:
                            c.start()
        return carry

    lax.fori_loop(1, 2 * nwin, both, 0)
    last_steps = feed(jnp.int32(2 * nwin - 1))
    for step in LAST:
        last_steps[step]()
    if remote:
        for c in halo:
            c.wait_send()
        for cs in back:
            for c in cs:
                c.wait()
    for j in range(ww):
        parts = [
            buf[2, 2 * j + b, 0:own, :].astype(F32).reshape(tile_rows, HALF, DIM) for b in range(2)
        ]
        out[:, j * WIN : (j + 1) * WIN, :] = jnp.concatenate(parts, axis=1).astype(BF16)


def body(remote, *args):
    tokens = args[0]
    tile_rows, tile_cols = tokens.shape[0], tokens.shape[1]
    ww = tile_cols // WIN
    vmem = pl.BlockSpec(memory_space=pltpu.VMEM)
    smem = pl.BlockSpec(memory_space=pltpu.SMEM)
    anym = pl.BlockSpec(memory_space=pl.ANY)
    return pl.pallas_call(
        functools.partial(kernel, remote),
        out_shape=jax.ShapeDtypeStruct(tokens.shape, BF16),
        in_specs=[anym, smem, anym, vmem, anym, vmem, anym, vmem, anym, vmem, vmem, vmem, smem, vmem],
        out_specs=vmem,
        scratch_shapes=[
            pltpu.VMEM(tokens.shape, BF16),
            pltpu.VMEM((2, DIM, 3 * DIM), BF16),
            pltpu.VMEM((2, DIM, DIM), BF16),
            pltpu.VMEM((2, DIM, FF), BF16),
            pltpu.VMEM((2, FF, DIM), BF16),
            pltpu.VMEM((3, 2 * ww + 1, (tile_rows + HALF) * HALF, DIM), BF16),
            pltpu.VMEM((2, HEADS, TOK, TOK), F32),
            pltpu.VMEM((2 * HEADS, LANES_POS), F32),
            pltpu.VMEM((2, 3 * 256, 128), F32),
            pltpu.VMEM((TOK, 4 * TOK), BF16),
            pltpu.VMEM((4 * TOK, 256), BF16),
            pltpu.VMEM((TOK, DIM), BF16),
            pltpu.VMEM((TOK, FF), BF16),
            pltpu.VMEM((256, 256), BF16),
            pltpu.VMEM((4, WIN, 128), BF16),
            pltpu.VMEM((4, TOK, 128), BF16),
            pltpu.VMEM((4, TOK, 128), BF16),
            pltpu.SemaphoreType.DMA((9,)),
            pltpu.SemaphoreType.DMA((9,)),
            pltpu.SemaphoreType.DMA((9,)),
        ],
        compiler_params=pltpu.CompilerParams(
            collective_id=0 if remote else None,
            has_side_effects=remote,
            vmem_limit_bytes=56 * 1024 * 1024,
        ),
    )(*args)


def solution(mesh):
    return jax.shard_map(
        functools.partial(body, True),
        mesh=mesh,
        in_specs=(P("row", "col", None), P("row", "col")) + (P(),) * 12,
        out_specs=P("row", "col", None),
        check_vma=False,
    )
```

time: 86.4 us -> 70.1 us (0.81)
  Pallas kernels: 82.8 us -> 67.2 us
    pallas_call x1, Pallas kernels: 82.8 us -> 67.2 us  [body(): pl.pallas_call(functools.partial(kernel, remote), out_shape=jax.ShapeDtyp...]
where the time goes in v2:
time: 70.1 us; the launch traced here: 69.9 us
  Pallas kernels  67.2 us (96%)
  local copies, waits for them, and re-layouts  2.66 us (4%)
    pallas_call x1, Pallas kernels, body(): pl.pallas_call(functools.partial(kernel, remote), out_shape=jax.ShapeDtyp...  67.2 us
    unnamed x1, local copies, waits for them, and re-layouts  2.66 us

profile of v2, /device:TPU:1, one launch (start us, length us, event | category | flops | bytes accessed | tf_op | source)
XLA Modules:
  0.0 69.9 jit_solution(9294986968000442634)
XLA Ops:
  0.0 67.2 %shard_map.136 = bf16[32,48,512]{2,1,0:T(8,128)(2,1)} custom-call(bf16[32,48,512]{2,1,0:T(8,128)(2,1)} %tok_hbm.1, s32[2,3]{1,0:T(2,128)} %mask.1, bf16[2,512,1536]{2,1,0:T(8,128)(2,1)} %wqkv_hbm.1, f32[2,1536]{1,0:T(2,128)} %bqkv.1, bf16[2,512,512]{2,1,0:T(8,128)(2,1)} %wproj_hbm.1, f32[2,512]{1,0:T(2,128)} %bproj.1, bf16[2,512,2048]{2,1,0:T(8,128)(2,1)} %wup_hbm.1, ...), custom_call_target="tpu_custom_call" | custom-call | tf_op jit(solution)/shard_map/pallas_call | solution.py:375
  67.2 2.7 %copy.16 = bf16[32,48,512]{2,1,0:T(8,128)(2,1)} copy(bf16[32,48,512]{2,1,0:T(8,128)(2,1)} %shard_map.136) | data formatting | bytes 3145728

commit v3 on v2

--- a/solution.py
+++ b/solution.py
@@ -20,28 +20,30 @@
 LOG2E = 1.4426950408889634
 LANES_POS = 1024
 CHUNK = 256
-ORDER = ((0, 1, 3, 2, 4, 5), (0, 3, 4, 5, 2, 1))
-HALO_AFTER = 2
-FIRST = [("start", 0)] + [(p, g) for g in range(2) for p in ("q", "k", "v", "unit")] + [("head", h) for h in range(16)]
-LAST = [("merge", 0), ("norm", 0)] + [("widen", f) for f in range(8)] + [("narrow", 0), ("narrow", 1), ("finish", 0)]
-OPENING = (
-    ("start", 0), ("q", 0), ("k", 0), ("merge", 0), ("v", 0), ("unit", 0), ("norm", 0),
-    ("q", 1), ("k", 1), ("v", 1),
+ORDER = ((0, 1, 3, 4, 2, 5), (0, 3, 2, 4, 5, 1))
+PROJECT = [("start", 0)] + [(p, g) for g in range(2) for p in ("q", "k", "v", "unit")]
+LAST = (
+    [("merge", 0)] + [("norm", c) for c in range(4)] + [("widen", f) for f in range(8)]
+    + [("narrow", 0), ("narrow", 1)] + [("finish", c) for c in range(4)]
 )
 AFTER = {
-    0: [("widen", 0)], 1: [("unit", 1), ("widen", 1), ("widen", 2)], 2: [("widen", 3)], 3: [("widen", 4)],
-    4: [("widen", 5), ("widen", 6)], 5: [("widen", 7), ("narrow", 0)], 6: [("narrow", 1)], 7: [("finish", 0)],
+    0: [("merge", 0)],
+    1: [("norm", 0), ("q", 0)],
+    2: [("norm", 1), ("k", 0)],
+    3: [("norm", 2), ("v", 0), ("unit", 0)],
+    4: [("norm", 3), ("q", 1)],
+    5: [("widen", 0), ("k", 1)],
+    6: [("widen", 1), ("v", 1), ("unit", 1)],
+    7: [("widen", 2)],
+    8: [("widen", 3), ("widen", 4)],
+    9: [("widen", 5)],
+    10: [("widen", 6)],
+    11: [("widen", 7), ("narrow", 0)],
+    12: [("narrow", 1)],
+    13: [("finish", 0)],
+    14: [("finish", 1), ("finish", 2)],
+    15: [("finish", 3)],
 }
-
-
-def mixed():
-    steps = list(OPENING)
-    for h in range(HEADS):
-        steps += [("head", h)] + AFTER.get(h, [])
-    return steps
-
-
-MIXED = mixed()
 
 GELU_POLY = (
     0.7978275766755302,
@@ -51,6 +53,7 @@
     1.1126326266502673e-06,
 )
 PENALTY = -30000.0
+ROWS = 64
 
 F32 = jnp.float32
 BF16 = jnp.bfloat16
@@ -62,34 +65,33 @@
 
 
 def twice_gelu(x):
-    u = x * x
-    p = GELU_POLY[-1]
+    v = x.astype(BF16)
+    u = v * v
+    p = jnp.asarray(GELU_POLY[-1], BF16)
     for c in GELU_POLY[-2::-1]:
-        p = p * u + c
-    return x * (jnp.tanh(x * p) + 1.0)
-
-
-def layer_norm(v, g, s):
+        p = p * u + jnp.asarray(c, BF16)
+    return x * (jnp.tanh(v * p).astype(F32) + 1.0)
+
+
+def layer_norm(v, g, s, eps):
     m = jnp.mean(v, axis=-1, keepdims=True)
     c = v - m
     var = jnp.mean(c * c, axis=-1, keepdims=True)
-    return c * lax.rsqrt(var + NORM_EPS) * g + s
+    return c * lax.rsqrt(var + eps) * g + s
 
 
 def spread_table(table, tscr, wscr):
     tscr[...] = jnp.zeros_like(tscr)
     for b in range(2):
-        tscr[b * HEADS : (b + 1) * HEADS, 0:POS] = table[b] * LOG2E
+        tscr[b * HEADS : (b + 1) * HEADS, 0:POS] = jnp.exp2(table[b] * LOG2E)
     t = tscr[...]
-    r = jnp.concatenate([pltpu.roll(t, LANES_POS - c, 1) if c else t for c in range(8)], axis=0)
-    hi = r.astype(BF16)
-    lo = (r - hi.astype(F32)).astype(BF16)
+    r = jnp.concatenate([pltpu.roll(t, LANES_POS - c, 1) if c else t for c in range(8)], axis=0).astype(BF16)
     rows = lax.broadcasted_iota(jnp.int32, (LANES_POS, 256), 0)
     lane = lax.broadcasted_iota(jnp.int32, (1, 256), 1)
     target = (30 - (lane >> 3)) * SPAN + 7 - (lane & 7)
     for d in range(3):
         pick = jnp.where(rows == target + 8 * d, 1.0, 0.0).astype(BF16)
-        w = dot(hi, pick) + dot(lo, pick)
+        w = dot(r, pick)
         for half in range(2):
             wscr[half, d * 256 : (d + 1) * 256, :] = w[:, half * 128 : (half + 1) * 128]
 
@@ -99,13 +101,15 @@
     for d in range(3):
         rows8 = pl.ds(d * 256 + b * HEADS + h, 8, stride=32)
         w0, w1 = wscr[0, rows8, :], wscr[1, rows8, :]
-        for rp in range(WIN):
-            o = (15 - rp) * 8
-            piece = pltpu.roll(jnp.where(lane < o, w1, w0), 128 - o, 1) if o else w0
+        for rp in range(0, WIN, 2):
+            pair = []
+            for o in ((15 - rp) * 8, (14 - rp) * 8):
+                pair.append(pltpu.roll(jnp.where(lane < o, w1, w0), 128 - o, 1) if o else w0)
+            piece = jnp.concatenate(pair, axis=0).astype(BF16)
             for bp in range(2):
                 bq = bp - (d - 1)
                 if 0 <= bq < 2:
-                    bias[b, h, bp * 128 + rp * 8 : bp * 128 + rp * 8 + 8, bq * 128 : bq * 128 + 128] = piece
+                    bias[b, h, bp * 128 + rp * 8 : bp * 128 + rp * 8 + 16, bq * 128 : bq * 128 + 128] = piece
 
 
 def kernel(
@@ -113,7 +117,7 @@
     tok_hbm, mask, wqkv_hbm, bqkv, wproj_hbm, bproj, wup_hbm, bup, wdown_hbm, bdown,
     gain, shift, lscale, table,
     out,
-    tok, wqkv, wproj, wup, wdown, buf, bias, tscr, wscr, prob, vone, ctx, hid, same, hmask, qlab, klab, load_sem, send_sem, recv_sem,
+    tok, wqkv, wproj, wup, wdown, buf, bias, tscr, wscr, prob, vone, ctx, hid, same, hmask, unit_qkv, qlab, klab, load_sem, send_sem, recv_sem,
 ):
     tile_rows, tile_cols = tok.shape[0], tok.shape[1]
     wh, ww = tile_rows // WIN, tile_cols // WIN
@@ -137,7 +141,6 @@
         barrier = pltpu.get_barrier_semaphore()
         for dev in ((up, col), (row, left), (up, left), (down, col), (row, right), (down, right)):
             pl.semaphore_signal(barrier, inc=1, device_id=dev, device_id_type=MESH)
-        pl.semaphore_wait(barrier, 6)
         last_row = row == nrow - 1
         last_col = col == ncol - 1
 
@@ -147,16 +150,17 @@
                 device_id=dev, device_id_type=MESH,
             )
 
-        first, second = buf.at[1], buf.at[2]
+        stage1, stage2 = buf.at[1], buf.at[2]
         inner = pl.ds(0, edge_rows)
         outer = pl.ds(own, edge_rows)
         halo = [
-            copy(0, first.at[pl.ds(0, halves), inner], first.at[pl.ds(0, halves), outer], (up, col)),
-            copy(1, first.at[0, pl.ds(0, own)], first.at[halves, pl.ds(0, own)], (row, left)),
-            copy(2, first.at[0, inner], first.at[halves, outer], (up, left)),
+            copy(0, stage1.at[pl.ds(0, halves - 2), inner], stage1.at[pl.ds(0, halves - 2), outer], (up, col)),
+            copy(1, stage1.at[0, pl.ds(0, own)], stage1.at[halves, pl.ds(0, own)], (row, left)),
+            copy(2, stage1.at[0, inner], stage1.at[halves, outer], (up, left)),
+            copy(3, stage1.at[pl.ds(halves - 2, 2), inner], stage1.at[pl.ds(halves - 2, 2), outer], (up, col)),
         ]
         back = [[] for _ in range(nwin)]
-        k = 3
+        k = 4
         for i in range(wh):
             for j in range(ww):
                 n = i * ww + j
@@ -166,14 +170,14 @@
                 if low:
                     cnt = 1 if right_edge else 2
                     cols = pl.ds(2 * j + 1, cnt)
-                    back[n].append(copy(k, second.at[cols, outer], second.at[cols, inner], (down, col)))
+                    back[n].append(copy(k, stage2.at[cols, outer], stage2.at[cols, inner], (down, col)))
                     k += 1
                 if right_edge:
                     rows = pl.ds(start, size)
-                    back[n].append(copy(k, second.at[halves, rows], second.at[0, rows], (row, right)))
+                    back[n].append(copy(k, stage2.at[halves, rows], stage2.at[0, rows], (row, right)))
                     k += 1
                 if low and right_edge:
-                    back[n].append(copy(k, second.at[halves, outer], second.at[0, inner], (down, right)))
+                    back[n].append(copy(k, stage2.at[halves, outer], stage2.at[0, inner], (down, right)))
                     k += 1
     else:
         last_row = last_col = jnp.bool_(False)
@@ -211,44 +215,53 @@
         i = idx // ww
         j = idx % ww
         cb = 2 * j + b
-        rows = pl.ds(pl.multiple_of(i * (TOK // 2) + b * edge_rows, edge_rows), TOK // 2)
-        return b, i, j, cb, rows
-
-    def load_x(b, cb, rows):
+        start = pl.multiple_of(i * (TOK // 2) + b * edge_rows, edge_rows)
+        return b, i, j, cb, start
+
+    def load_x(b, cb, start):
+        rows = pl.ds(start, TOK // 2)
         return jnp.concatenate([buf[b, cb, rows, :], buf[b, cb + 1, rows, :]], axis=0)
 
     def attention(w):
-        b, i, j, cb, rows = place(w)
+        b, i, j, cb, start = place(w)
         st = {}
 
-        def start():
-            st["x"] = load_x(b, cb, rows)
+        def begin():
+            st["x"] = load_x(b, cb, start)
             sc = jnp.zeros((1, DIM), F32)
             for h in range(HEADS):
                 sc = jnp.where((lane512 >> 5) == h, lscale[b, h] * LOG2E, sc)
             st["sc"] = sc
+
+        def fetch():
             cut_row = jnp.logical_and(jnp.logical_and(last_row, b == 1), i == wh - 1)
             cut_col = jnp.logical_and(jnp.logical_and(last_col, b == 1), j == ww - 1)
             st["case"] = cut_row.astype(jnp.int32) * 2 + cut_col.astype(jnp.int32)
+            for g in range(2):
+                for n, name in enumerate(("qn", "kn", "vn")):
+                    st[name, g] = unit_qkv[n, g]
 
         def project(part, g):
             lanes = slice(part * DIM + g * 256, part * DIM + (g + 1) * 256)
             r = dot(st["x"], wqkv[b, :, lanes]) + bqkv[pl.ds(b, 1), lanes]
-            st[part, g] = r.astype(BF16) if part == 2 else r
+            if part == 2:
+                unit_qkv[2, g] = r.astype(BF16)
+            else:
+                st[part, g] = r
 
         def unit(g):
             lanes = slice(g * 256, (g + 1) * 256)
             qg, kg = st[0, g], st[1, g]
             q2 = dot((qg * qg).astype(BF16), same[...])
             k2 = dot((kg * kg).astype(BF16), same[...])
-            st["qn", g] = (qg * (lax.rsqrt(jnp.maximum(q2, 1.0)) * st["sc"][:, lanes])).astype(BF16)
-            st["kn", g] = (kg * lax.rsqrt(jnp.maximum(k2, 1.0))).astype(BF16)
+            unit_qkv[0, g] = (qg * (lax.rsqrt(jnp.maximum(q2, 1.0)) * st["sc"][:, lanes])).astype(BF16)
+            unit_qkv[1, g] = (kg * lax.rsqrt(jnp.maximum(k2, 1.0))).astype(BF16)
 
         def head(h):
             h4, g = h % 4, h // 8
             here = slice((h - h4) % 8 * HEAD_DIM, (h - h4) % 8 * HEAD_DIM + 128)
             only = hmask[h4][None]
-            vg = st[2, g][:, here].reshape(WIN, WIN, 128)
+            vg = st["vn", g][:, here].reshape(WIN, WIN, 128)
             vone[h4 * TOK : (h4 + 1) * TOK, 0:128] = (vg * only).reshape(TOK, 128)
             qm = (st["qn", g][:, here].reshape(WIN, WIN, 128) * only).reshape(TOK, 128)
             s = lax.dot_general(
@@ -256,13 +269,13 @@
                 jnp.concatenate([st["kn", g][:, here], klab[st["case"]]], axis=1),
                 (((1,), (1,)), ((), ())), preferred_element_type=F32,
             )
-            prob[:, h4 * TOK : (h4 + 1) * TOK] = jnp.exp2(s + bias[b, h]).astype(BF16)
+            prob[:, h4 * TOK : (h4 + 1) * TOK] = jnp.exp2(s).astype(BF16) * bias[b, h]
             if h4 == 3:
                 o = dot(prob[...], vone[...])
                 v0 = (h - 3) * HEAD_DIM
                 ctx[:, v0 : v0 + 128] = (o[:, 0:128] * pl.reciprocal(o[:, 128:256], approx=True)).astype(BF16)
 
-        steps = {("start", 0): start}
+        steps = {("start", 0): begin, ("fetch", 0): fetch}
         for g in range(2):
             steps["unit", g] = functools.partial(unit, g)
             for part in range(3):
@@ -272,16 +285,19 @@
         return steps
 
     def feed(w):
-        b, i, j, cb, rows = place(w)
+        b, i, j, cb, start = place(w)
         st = {}
 
         def merge():
-            st["x"] = load_x(b, cb, rows).astype(F32)
+            st["x"] = load_x(b, cb, start).astype(F32)
             st["att"] = dot(ctx[...], wproj[b]) + bproj[pl.ds(b, 1), :]
 
-        def norm():
-            mid = st["x"] + layer_norm(st["att"], gain[b, 0:1, :], shift[b, 0:1, :])
-            st["mid"] = mid.astype(BF16)
+        def norm(c):
+            part = slice(c * ROWS, (c + 1) * ROWS)
+            mid = st["x"][part] + layer_norm(st["att"][part], gain[b, 0:1, :], shift[b, 0:1, :], NORM_EPS)
+            st["mid", c] = mid.astype(BF16)
+            if c == TOK // ROWS - 1:
+                st["mid"] = jnp.concatenate([st["mid", k] for k in range(TOK // ROWS)], axis=0)
 
         def widen(f):
             lanes = slice(f * CHUNK, (f + 1) * CHUNK)
@@ -290,16 +306,21 @@
 
         def narrow(n):
             lanes = slice(n * 256, (n + 1) * 256)
-            st["red", n] = 0.5 * dot(hid[...], wdown[b, :, lanes]) + bdown[pl.ds(b, 1), lanes]
-
-        def finish():
-            y = st["mid"].astype(F32) + layer_norm(jnp.concatenate([st["red", 0], st["red", 1]], axis=1), gain[b, 1:2, :], shift[b, 1:2, :])
+            st["red", n] = dot(hid[...], wdown[b, :, lanes]) + 2.0 * bdown[pl.ds(b, 1), lanes]
+
+        def finish(c):
+            part = slice(c * ROWS, (c + 1) * ROWS)
+            red = jnp.concatenate([st["red", 0][part], st["red", 1][part]], axis=1)
+            y = st["mid", c].astype(F32) + layer_norm(red, gain[b, 1:2, :], shift[b, 1:2, :], 4.0 * NORM_EPS)
             keep = jnp.logical_or(mask[i, j] == 1, b == 1)
-            y = jnp.where(keep, y, st["x"]).astype(BF16)
-            buf[b + 1, cb, rows, :] = y[0 : TOK // 2]
-            buf[b + 1, cb + 1, rows, :] = y[TOK // 2 :]
-
-        steps = {("merge", 0): merge, ("norm", 0): norm, ("finish", 0): finish}
+            y = jnp.where(keep, y, st["x"][part]).astype(BF16)
+            per = TOK // 2 // ROWS
+            buf[b + 1, cb + c // per, pl.ds(pl.multiple_of(start + c % per * ROWS, ROWS), ROWS), :] = y
+
+        steps = {("merge", 0): merge}
+        for c in range(TOK // ROWS):
+            steps["norm", c] = functools.partial(norm, c)
+            steps["finish", c] = functools.partial(finish, c)
         for f in range(FF // CHUNK):
             steps["widen", f] = functools.partial(widen, f)
         for n in range(2):
@@ -310,36 +331,61 @@
         c.wait()
     for c in loads[1]:
         c.start()
-    first_steps = attention(jnp.int32(0))
-    for step in FIRST:
-        if step[0] == "head":
-            for b in range(2):
-                expand_bias(wscr, bias, b, step[1])
-        first_steps[step]()
+    first, ahead = attention(jnp.int32(0)), attention(jnp.int32(1))
+    for step in PROJECT:
+        first[step]()
+    first["fetch", 0]()
+    for h in range(HEADS):
+        for b in range(2):
+            expand_bias(wscr, bias, b, h)
+        first["head", h]()
+    for step in PROJECT:
+        ahead[step]()
 
     def both(t, carry):
-        @pl.when(t == nwin)
+        @pl.when(t == nwin - 1)
         def _():
             for c in loads[1]:
                 c.wait()
 
         if remote:
+            @pl.when(t == nwin)
+            def _():
+                halo[0].wait_recv()
+
             @pl.when(t == nwin + 1)
             def _():
-                for c in halo:
-                    c.wait_recv()
-
-        steps = {**attention(t), **feed(t - 1)}
-        for step in MIXED:
-            steps[step]()
+                halo[1].wait_recv()
+
+            @pl.when(t == nwin + 2)
+            def _():
+                halo[2].wait_recv()
+                halo[3].wait_recv()
+
+        now, ahead, behind = attention(t), attention(jnp.minimum(t + 1, 2 * nwin - 1)), feed(t - 1)
+        now["fetch", 0]()
+        ahead["start", 0]()
+        for h in range(HEADS):
+            now["head", h]()
+            for step in AFTER.get(h, ()):
+                (behind if step in behind else ahead)[step]()
 
         if remote:
+            @pl.when(t == 2)
+            def _():
+                pl.semaphore_wait(barrier, 6)
+                halo[0].start()
+
+            @pl.when(t == 3)
+            def _():
+                halo[1].start()
+                halo[2].start()
+
+            @pl.when(t == 5)
+            def _():
+                halo[3].start()
+
             for pos in range(nwin):
-                if ORDER[0][pos] == HALO_AFTER:
-                    @pl.when(t == pos + 1)
-                    def _():
-                        for c in halo:
-                            c.start()
                 n_ = ORDER[1][pos]
                 if back[n_] and pos < nwin - 1:
                     @pl.when(t == nwin + pos + 1)
@@ -384,7 +430,7 @@
             pltpu.VMEM((2, DIM, FF), BF16),
             pltpu.VMEM((2, FF, DIM), BF16),
             pltpu.VMEM((3, 2 * ww + 1, (tile_rows + HALF) * HALF, DIM), BF16),
-            pltpu.VMEM((2, HEADS, TOK, TOK), F32),
+            pltpu.VMEM((2, HEADS, TOK, TOK), BF16),
             pltpu.VMEM((2 * HEADS, LANES_POS), F32),
             pltpu.VMEM((2, 3 * 256, 128), F32),
             pltpu.VMEM((TOK, 4 * TOK), BF16),
@@ -393,11 +439,12 @@
             pltpu.VMEM((TOK, FF), BF16),
             pltpu.VMEM((256, 256), BF16),
             pltpu.VMEM((4, WIN, 128), BF16),
+            pltpu.VMEM((3, 2, TOK, 256), BF16),
             pltpu.VMEM((4, TOK, 128), BF16),
             pltpu.VMEM((4, TOK, 128), BF16),
             pltpu.SemaphoreType.DMA((9,)),
-            pltpu.SemaphoreType.DMA((9,)),
-            pltpu.SemaphoreType.DMA((9,)),
+            pltpu.SemaphoreType.DMA((10,)),
+            pltpu.SemaphoreType.DMA((10,)),
         ],
         compiler_params=pltpu.CompilerParams(
             collective_id=0 if remote else None,

time: 70.1 us -> 66.2 us (0.944); the launches traced: 69.9 us -> 65.2 us
  Pallas kernels: 67.2 us -> 62.5 us
    pallas_call x1, Pallas kernels: 67.2 us -> 62.5 us  [body(): pl.pallas_call(functools.partial(kernel, remote), out_shape=jax.ShapeDtyp...]
where the time goes in v3:
time: 66.2 us; the launch traced here: 65.2 us
  Pallas kernels  62.5 us (94%)
  local copies, waits for them, and re-layouts  2.66 us (4%)
    pallas_call x1, Pallas kernels, body(): pl.pallas_call(functools.partial(kernel, remote), out_shape=jax.ShapeDtyp...  62.5 us
    unnamed x1, local copies, waits for them, and re-layouts  2.66 us

profile of v3, /device:TPU:1, one launch (start us, length us, event | category | flops | bytes accessed | tf_op | source)
XLA Modules:
  0.0 65.2 jit_solution(2260742540989632485)
XLA Ops:
  0.0 62.5 %shard_map.136 = bf16[32,48,512]{2,1,0:T(8,128)(2,1)} custom-call(bf16[32,48,512]{2,1,0:T(8,128)(2,1)} %tok_hbm.1, s32[2,3]{1,0:T(2,128)} %mask.1, bf16[2,512,1536]{2,1,0:T(8,128)(2,1)} %wqkv_hbm.1, f32[2,1536]{1,0:T(2,128)} %bqkv.1, bf16[2,512,512]{2,1,0:T(8,128)(2,1)} %wproj_hbm.1, f32[2,512]{1,0:T(2,128)} %bproj.1, bf16[2,512,2048]{2,1,0:T(8,128)(2,1)} %wup_hbm.1, ...), custom_call_target="tpu_custom_call" | custom-call | tf_op jit(solution)/shard_map/pallas_call | solution.py:421
  62.6 2.7 %copy.16 = bf16[32,48,512]{2,1,0:T(8,128)(2,1)} copy(bf16[32,48,512]{2,1,0:T(8,128)(2,1)} %shard_map.136) | data formatting | bytes 3145728

commit v4 on v3

--- a/solution.py
+++ b/solution.py
@@ -26,23 +26,26 @@
     [("merge", 0)] + [("norm", c) for c in range(4)] + [("widen", f) for f in range(8)]
     + [("narrow", 0), ("narrow", 1)] + [("finish", c) for c in range(4)]
 )
+SPREAD = {
+    1: [("start", 0), ("q", 0)], 3: [("k", 0)], 5: [("v", 0)], 7: [("unit", 0)], 9: [("q", 1)], 11: [("k", 1)], 13: [("v", 1)], 14: [("unit", 1)],
+}
 AFTER = {
-    0: [("merge", 0)],
-    1: [("norm", 0), ("q", 0)],
-    2: [("norm", 1), ("k", 0)],
-    3: [("norm", 2), ("v", 0), ("unit", 0)],
-    4: [("norm", 3), ("q", 1)],
-    5: [("widen", 0), ("k", 1)],
-    6: [("widen", 1), ("v", 1), ("unit", 1)],
-    7: [("widen", 2)],
-    8: [("widen", 3), ("widen", 4)],
+    0: [("merge", 0), ("q", 0)],
+    1: [("norm", 0), ("k", 0)],
+    2: [("norm", 1), ("v", 0), ("unit", 0)],
+    3: [("norm", 2), ("norm", 3), ("q", 1)],
+    4: [("widen", 0), ("k", 1)],
+    5: [("widen", 1)],
+    6: [("widen", 2)],
+    7: [("widen", 3)],
+    8: [("widen", 4)],
     9: [("widen", 5)],
     10: [("widen", 6)],
-    11: [("widen", 7), ("narrow", 0)],
-    12: [("narrow", 1)],
-    13: [("finish", 0)],
-    14: [("finish", 1), ("finish", 2)],
-    15: [("finish", 3)],
+    11: [("widen", 7)],
+    12: [("narrow", 0)],
+    13: [("narrow", 1), ("finish", 0)],
+    14: [("finish", 1), ("finish", 2), ("v", 1)],
+    15: [("finish", 3), ("unit", 1)],
 }
 
 GELU_POLY = (
@@ -54,6 +57,7 @@
 )
 PENALTY = -30000.0
 ROWS = 64
+OUT_ROWS = 16
 
 F32 = jnp.float32
 BF16 = jnp.bfloat16
@@ -70,7 +74,7 @@
     p = jnp.asarray(GELU_POLY[-1], BF16)
     for c in GELU_POLY[-2::-1]:
         p = p * u + jnp.asarray(c, BF16)
-    return x * (jnp.tanh(v * p).astype(F32) + 1.0)
+    return v * (jnp.tanh(v * p) + jnp.asarray(1.0, BF16))
 
 
 def layer_norm(v, g, s, eps):
@@ -117,7 +121,7 @@
     tok_hbm, mask, wqkv_hbm, bqkv, wproj_hbm, bproj, wup_hbm, bup, wdown_hbm, bdown,
     gain, shift, lscale, table,
     out,
-    tok, wqkv, wproj, wup, wdown, buf, bias, tscr, wscr, prob, vone, ctx, hid, same, hmask, unit_qkv, qlab, klab, load_sem, send_sem, recv_sem,
+    tok, wqkv, wproj, wup, wdown, buf, bias, tscr, wscr, prob, vone, ctx, hid, same, hmask, unit_qkv, qlab, klab, load_sem, out_sem, send_sem, recv_sem,
 ):
     tile_rows, tile_cols = tok.shape[0], tok.shape[1]
     wh, ww = tile_rows // WIN, tile_cols // WIN
@@ -339,8 +343,8 @@
         for b in range(2):
             expand_bias(wscr, bias, b, h)
         first["head", h]()
-    for step in PROJECT:
-        ahead[step]()
+        for step in SPREAD.get(h, ()):
+            ahead[step]()
 
     def both(t, carry):
         @pl.when(t == nwin - 1)
@@ -398,17 +402,31 @@
     last_steps = feed(jnp.int32(2 * nwin - 1))
     for step in LAST:
         last_steps[step]()
+    inside, below = pl.ds(edge_rows, own - edge_rows), pl.ds(0, edge_rows)
+    later = pl.ds(1, halves - 1)
+    outs = [
+        pltpu.make_async_copy(buf.at[2, later, inside], out.at[later, inside], out_sem.at[0]),
+        pltpu.make_async_copy(buf.at[2, later, below], out.at[later, below], out_sem.at[1]),
+        pltpu.make_async_copy(buf.at[2, 0, pl.ds(0, own)], out.at[0], out_sem.at[2]),
+    ]
+    outs[0].start()
     if remote:
         for c in halo:
             c.wait_send()
         for cs in back:
             for c in cs:
                 c.wait()
-    for j in range(ww):
-        parts = [
-            buf[2, 2 * j + b, 0:own, :].astype(F32).reshape(tile_rows, HALF, DIM) for b in range(2)
-        ]
-        out[:, j * WIN : (j + 1) * WIN, :] = jnp.concatenate(parts, axis=1).astype(BF16)
+    outs[1].start()
+    outs[2].start()
+    for c in outs:
+        c.wait()
+
+
+def assemble(halves_ref, out_ref):
+    rows = out_ref.shape[0]
+    for j in range(out_ref.shape[1] // WIN):
+        parts = [halves_ref[2 * j + b].astype(F32).reshape(rows, HALF, DIM) for b in range(2)]
+        out_ref[:, j * WIN : (j + 1) * WIN, :] = jnp.concatenate(parts, axis=1).astype(BF16)
 
 
 def body(remote, *args):
@@ -418,11 +436,12 @@
     vmem = pl.BlockSpec(memory_space=pltpu.VMEM)
     smem = pl.BlockSpec(memory_space=pltpu.SMEM)
     anym = pl.BlockSpec(memory_space=pl.ANY)
-    return pl.pallas_call(
+    halves = 2 * ww
+    encoded = pl.pallas_call(
         functools.partial(kernel, remote),
-        out_shape=jax.ShapeDtypeStruct(tokens.shape, BF16),
+        out_shape=jax.ShapeDtypeStruct((halves, tile_rows * HALF, DIM), BF16),
         in_specs=[anym, smem, anym, vmem, anym, vmem, anym, vmem, anym, vmem, vmem, vmem, smem, vmem],
-        out_specs=vmem,
+        out_specs=anym,
         scratch_shapes=[
             pltpu.VMEM(tokens.shape, BF16),
             pltpu.VMEM((2, DIM, 3 * DIM), BF16),
@@ -443,6 +462,7 @@
             pltpu.VMEM((4, TOK, 128), BF16),
             pltpu.VMEM((4, TOK, 128), BF16),
             pltpu.SemaphoreType.DMA((9,)),
+            pltpu.SemaphoreType.DMA((3,)),
             pltpu.SemaphoreType.DMA((10,)),
             pltpu.SemaphoreType.DMA((10,)),
         ],
@@ -452,6 +472,13 @@
             vmem_limit_bytes=56 * 1024 * 1024,
         ),
     )(*args)
+    return pl.pallas_call(
+        assemble,
+        grid=(tile_rows // OUT_ROWS,),
+        out_shape=jax.ShapeDtypeStruct(tokens.shape, BF16),
+        in_specs=[pl.BlockSpec((halves, OUT_ROWS * HALF, DIM), lambda i: (0, i, 0))],
+        out_specs=pl.BlockSpec((OUT_ROWS, tile_cols, DIM), lambda i: (i, 0, 0)),
+    )(encoded)
 
 
 def solution(mesh):

time: 66.2 us -> 62.3 us (0.941)
  local copies, waits for them, and re-layouts: 2.66 us -> 0 us
  Pallas kernels: 62.5 us -> 61.2 us
    pallas_call x1, Pallas kernels: 62.5 us -> 58.9 us  [body(): pl.pallas_call(functools.partial(kernel, remote), out_shape=jax.ShapeDtyp...]
    unnamed x1 -> x0, local copies, waits for them, and re-layouts: 2.66 us -> none
    pallas_call x0 -> x1, Pallas kernels: none -> 2.34 us  [body(): pl.pallas_call(assemble, grid=(tile_rows // OUT_ROWS,), out_shape=jax.Sha...]
where the time goes in v4:
time: 62.3 us; the launch traced here: 61.2 us
  Pallas kernels  61.2 us (98%)
    pallas_call x1, Pallas kernels, body(): pl.pallas_call(functools.partial(kernel, remote), out_shape=jax.ShapeDtyp...  58.9 us
    pallas_call x1, Pallas kernels, body(): pl.pallas_call(assemble, grid=(tile_rows // OUT_ROWS,), out_shape=jax.Sha...  2.34 us

profile of v4, /device:TPU:1, one launch (start us, length us, event | category | flops | bytes accessed | tf_op | source)
XLA Modules:
  0.0 61.2 jit_solution(7763657386076847677)
XLA Ops:
  0.0 58.9 %shard_map.136.halves_ref = bf16[6,256,512]{2,1,0:T(8,128)(2,1)} custom-call(bf16[32,48,512]{2,1,0:T(8,128)(2,1)} %tok_hbm.1, s32[2,3]{1,0:T(2,128)} %mask.1, bf16[2,512,1536]{2,1,0:T(8,128)(2,1)} %wqkv_hbm.1, f32[2,1536]{1,0:T(2,128)} %bqkv.1, bf16[2,512,512]{2,1,0:T(8,128)(2,1)} %wproj_hbm.1, f32[2,512]{1,0:T(2,128)} %bproj.1, ...), custom_call_target="tpu_custom_call" | custom-call | tf_op jit(solution)/shard_map/pallas_call | solution.py:440
  58.9 2.3 %shard_map.137 = bf16[32,48,512]{2,1,0:T(8,128)(2,1)} custom-call(bf16[6,256,512]{2,1,0:T(8,128)(2,1)} %shard_map.136.halves_ref), custom_call_target="tpu_custom_call" | custom-call | tf_op jit(solution)/shard_map/pallas_call | solution.py:475

commit v5 on v4

--- a/solution.py
+++ b/solution.py
@@ -20,7 +20,7 @@
 LOG2E = 1.4426950408889634
 LANES_POS = 1024
 CHUNK = 256
-ORDER = ((0, 1, 3, 4, 2, 5), (0, 3, 2, 4, 5, 1))
+ORDER = ((0, 3, 2, 5, 1, 4), (2, 5, 3, 4, 0, 1))
 PROJECT = [("start", 0)] + [(p, g) for g in range(2) for p in ("q", "k", "v", "unit")]
 LAST = (
     [("merge", 0)] + [("norm", c) for c in range(4)] + [("widen", f) for f in range(8)]
@@ -157,14 +157,19 @@
         stage1, stage2 = buf.at[1], buf.at[2]
         inner = pl.ds(0, edge_rows)
         outer = pl.ds(own, edge_rows)
+        def to_above(k, j):
+            cols = pl.ds(2 * j, 2)
+            return copy(k, stage1.at[cols, inner], stage1.at[cols, outer], (up, col))
+
         halo = [
-            copy(0, stage1.at[pl.ds(0, halves - 2), inner], stage1.at[pl.ds(0, halves - 2), outer], (up, col)),
-            copy(1, stage1.at[0, pl.ds(0, own)], stage1.at[halves, pl.ds(0, own)], (row, left)),
-            copy(2, stage1.at[0, inner], stage1.at[halves, outer], (up, left)),
-            copy(3, stage1.at[pl.ds(halves - 2, 2), inner], stage1.at[pl.ds(halves - 2, 2), outer], (up, col)),
+            to_above(0, 0),
+            to_above(1, 1),
+            to_above(2, 2),
+            copy(3, stage1.at[0, pl.ds(0, own)], stage1.at[halves, pl.ds(0, own)], (row, left)),
+            copy(4, stage1.at[0, inner], stage1.at[halves, outer], (up, left)),
         ]
         back = [[] for _ in range(nwin)]
-        k = 4
+        k = 5
         for i in range(wh):
             for j in range(ww):
                 n = i * ww + j
@@ -353,18 +358,19 @@
                 c.wait()
 
         if remote:
+            @pl.when(t == nwin - 1)
+            def _():
+                halo[3].wait_recv()
+
             @pl.when(t == nwin)
             def _():
+                halo[2].wait_recv()
+                halo[4].wait_recv()
+
+            @pl.when(t == nwin + 1)
+            def _():
                 halo[0].wait_recv()
-
-            @pl.when(t == nwin + 1)
-            def _():
                 halo[1].wait_recv()
-
-            @pl.when(t == nwin + 2)
-            def _():
-                halo[2].wait_recv()
-                halo[3].wait_recv()
 
         now, ahead, behind = attention(t), attention(jnp.minimum(t + 1, 2 * nwin - 1)), feed(t - 1)
         now["fetch", 0]()
@@ -378,16 +384,16 @@
             @pl.when(t == 2)
             def _():
                 pl.semaphore_wait(barrier, 6)
-                halo[0].start()
+                for k in (3, 4, 0):
+                    halo[k].start()
 
             @pl.when(t == 3)
             def _():
+                halo[2].start()
+
+            @pl.when(t == 5)
+            def _():
                 halo[1].start()
-                halo[2].start()
-
-            @pl.when(t == 5)
-            def _():
-                halo[3].start()
 
             for pos in range(nwin):
                 n_ = ORDER[1][pos]
@@ -463,8 +469,8 @@
             pltpu.VMEM((4, TOK, 128), BF16),
             pltpu.SemaphoreType.DMA((9,)),
             pltpu.SemaphoreType.DMA((3,)),
-            pltpu.SemaphoreType.DMA((10,)),
-            pltpu.SemaphoreType.DMA((10,)),
+            pltpu.SemaphoreType.DMA((11,)),
+            pltpu.SemaphoreType.DMA((11,)),
         ],
         compiler_params=pltpu.CompilerParams(
             collective_id=0 if remote else None,

time: 62.3 us -> 57.5 us (0.923); the launches traced: 61.2 us -> 57.3 us
  Pallas kernels: 61.2 us -> 57.3 us
    pallas_call x1, Pallas kernels: 58.9 us -> 55 us  [body(): pl.pallas_call(functools.partial(kernel, remote), out_shape=jax.ShapeDtyp...]
where the time goes in v5:
time: 57.5 us; the launch traced here: 57.3 us
  Pallas kernels  57.3 us (100%)
    pallas_call x1, Pallas kernels, body(): pl.pallas_call(functools.partial(kernel, remote), out_shape=jax.ShapeDtyp...  55 us
    pallas_call x1, Pallas kernels, body(): pl.pallas_call(assemble, grid=(tile_rows // OUT_ROWS,), out_shape=jax.Sha...  2.34 us

profile of v5, /device:TPU:1, one launch (start us, length us, event | category | flops | bytes accessed | tf_op | source)
XLA Modules:
  0.0 57.3 jit_solution(4940114422109492208)
XLA Ops:
  0.0 55.0 %shard_map.136.halves_ref = bf16[6,256,512]{2,1,0:T(8,128)(2,1)} custom-call(bf16[32,48,512]{2,1,0:T(8,128)(2,1)} %tok_hbm.1, s32[2,3]{1,0:T(2,128)} %mask.1, bf16[2,512,1536]{2,1,0:T(8,128)(2,1)} %wqkv_hbm.1, f32[2,1536]{1,0:T(2,128)} %bqkv.1, bf16[2,512,512]{2,1,0:T(8,128)(2,1)} %wproj_hbm.1, f32[2,512]{1,0:T(2,128)} %bproj.1, ...), custom_call_target="tpu_custom_call" | custom-call | tf_op jit(solution)/shard_map/pallas_call | solution.py:446
  55.0 2.3 %shard_map.137 = bf16[32,48,512]{2,1,0:T(8,128)(2,1)} custom-call(bf16[6,256,512]{2,1,0:T(8,128)(2,1)} %shard_map.136.halves_ref), custom_call_target="tpu_custom_call" | custom-call | tf_op jit(solution)/shard_map/pallas_call | solution.py:481

commit v6 on v5

--- a/solution.py
+++ b/solution.py
@@ -372,7 +372,7 @@
                 halo[0].wait_recv()
                 halo[1].wait_recv()
 
-        now, ahead, behind = attention(t), attention(jnp.minimum(t + 1, 2 * nwin - 1)), feed(t - 1)
+        now, ahead, behind = attention(t), attention(t + 1), feed(t - 1)
         now["fetch", 0]()
         ahead["start", 0]()
         for h in range(HEADS):
@@ -404,26 +404,41 @@
                             c.start()
         return carry
 
-    lax.fori_loop(1, 2 * nwin, both, 0)
-    last_steps = feed(jnp.int32(2 * nwin - 1))
+    lax.fori_loop(1, 2 * nwin - 1, both, 0)
+    now, behind, last = attention(jnp.int32(2 * nwin - 1)), feed(jnp.int32(2 * nwin - 2)), feed(jnp.int32(2 * nwin - 1))
+    now["fetch", 0]()
+    for h in range(HEADS):
+        now["head", h]()
+        for step in AFTER.get(h, ()):
+            if step in behind:
+                behind[step]()
+
+    column = 2 * (ORDER[1][-1] % ww) + 1
+    inside, below = pl.ds(edge_rows, own - edge_rows), pl.ds(0, edge_rows)
+    window_rows = pl.ds(edge_rows, TOK // 2)
+    under = pl.ds(edge_rows + TOK // 2, own - edge_rows - TOK // 2)
+    here = pl.ds(column, 2)
+    places = (
+        (pl.ds(1, column - 1), inside), (pl.ds(column + 2, halves - column - 2), inside), (here, under),
+        (here, window_rows), (pl.ds(1, halves - 1), below), (pl.ds(0, 1), pl.ds(0, own)),
+    )
+    outs = [
+        pltpu.make_async_copy(buf.at[2, cols, rows], out.at[cols, rows], out_sem.at[k])
+        for k, (cols, rows) in enumerate(places)
+    ]
+    for c in outs[:3]:
+        c.start()
     for step in LAST:
-        last_steps[step]()
-    inside, below = pl.ds(edge_rows, own - edge_rows), pl.ds(0, edge_rows)
-    later = pl.ds(1, halves - 1)
-    outs = [
-        pltpu.make_async_copy(buf.at[2, later, inside], out.at[later, inside], out_sem.at[0]),
-        pltpu.make_async_copy(buf.at[2, later, below], out.at[later, below], out_sem.at[1]),
-        pltpu.make_async_copy(buf.at[2, 0, pl.ds(0, own)], out.at[0], out_sem.at[2]),
-    ]
-    outs[0].start()
+        last[step]()
+    outs[3].start()
     if remote:
         for c in halo:
             c.wait_send()
         for cs in back:
             for c in cs:
                 c.wait()
-    outs[1].start()
-    outs[2].start()
+    for c in outs[4:]:
+        c.start()
     for c in outs:
         c.wait()
 
@@ -468,7 +483,7 @@
             pltpu.VMEM((4, TOK, 128), BF16),
             pltpu.VMEM((4, TOK, 128), BF16),
             pltpu.SemaphoreType.DMA((9,)),
-            pltpu.SemaphoreType.DMA((3,)),
+            pltpu.SemaphoreType.DMA((6,)),
             pltpu.SemaphoreType.DMA((11,)),
             pltpu.SemaphoreType.DMA((11,)),
         ],

time: 57.5 us -> 57.1 us (level)
  no operation moved by 1% of the time
where the time goes in v6:
time: 57.1 us; the launch traced here: 56.9 us
  Pallas kernels  56.9 us (100%)
    pallas_call x1, Pallas kernels, body(): pl.pallas_call(functools.partial(kernel, remote), out_shape=jax.ShapeDtyp...  54.6 us
    pallas_call x1, Pallas kernels, body(): pl.pallas_call(assemble, grid=(tile_rows // OUT_ROWS,), out_shape=jax.Sha...  2.34 us

profile of v6, /device:TPU:1, one launch (start us, length us, event | category | flops | bytes accessed | tf_op | source)
XLA Modules:
  0.0 56.9 jit_solution(14312285531165680910)
XLA Ops:
  0.0 54.6 %shard_map.136.halves_ref = bf16[6,256,512]{2,1,0:T(8,128)(2,1)} custom-call(bf16[32,48,512]{2,1,0:T(8,128)(2,1)} %tok_hbm.1, s32[2,3]{1,0:T(2,128)} %mask.1, bf16[2,512,1536]{2,1,0:T(8,128)(2,1)} %wqkv_hbm.1, f32[2,1536]{1,0:T(2,128)} %bqkv.1, bf16[2,512,512]{2,1,0:T(8,128)(2,1)} %wproj_hbm.1, f32[2,512]{1,0:T(2,128)} %bproj.1, ...), custom_call_target="tpu_custom_call" | custom-call | tf_op jit(solution)/shard_map/pallas_call | solution.py:461
  54.6 2.3 %shard_map.137 = bf16[32,48,512]{2,1,0:T(8,128)(2,1)} custom-call(bf16[6,256,512]{2,1,0:T(8,128)(2,1)} %shard_map.136.halves_ref), custom_call_target="tpu_custom_call" | custom-call | tf_op jit(solution)/shard_map/pallas_call | solution.py:496
